TPU v7x, 256 devices: a whole 4x4x8 slice. The times are simulated.
256 devices in a mesh: lat: 8 (over y_lo, x), lon: 32 (over y_hi, z, core).
Axes of the slice: x: 4, y: 4 (y_hi: 2, y_lo: 2; y = y_hi * 2 + y_lo), z: 8, core: 2. Of those that a mesh axis runs over, the one named last changes fastest.
Arguments:
- queries: bfloat16 [64, 1024, 512], P('lat', 'lon'), may hold values from -8 to 8
- keys: bfloat16 [64, 1024, 512], P('lat', 'lon'), may hold values from -8 to 8
- values: bfloat16 [64, 1024, 512], P('lat', 'lon'), may hold values from -6 to 6
- grad_out: bfloat16 [64, 1024, 512], P('lat', 'lon'), may hold values from -6 to 6
- sink_logits: float32 [8], replicated, may hold values from 4 to 8
Outputs:
- attended: bfloat16 [64, 1024, 512], P('lat', 'lon')
- query_grad: bfloat16 [64, 1024, 512], P('lat', 'lon')
- key_grad: bfloat16 [64, 1024, 512], P('lat', 'lon')
- value_grad: bfloat16 [64, 1024, 512], P('lat', 'lon')
- sink_grad: float32 [8], replicated
All inputs are finite; a program needn't handle non-finite values.
Results may differ from a plain program's by a relative error of at most 0.0085.
Values may be sent and summed in bfloat16 or wider, within the bound.
A program may use at most 64 MiB of HBM per device.

v0:
```python
import math

import jax
import jax.numpy as jnp
from jax import lax
from jax.sharding import PartitionSpec as P

WIN = 13


softcap = 8.0


def shifted(value, axis, by):
    size = lax.axis_size(axis)
    return lax.ppermute(value, axis, [(i, (i + by) % size) for i in range(size)])


def shifted_2(value, axis, by):
    size = lax.axis_size(axis)
    pairs = [(i, i + by) for i in range(size) if 0 <= i + by < size]
    return lax.ppermute(value, axis, pairs)


def extended_2(cells, sides, width, closed):
    for axis, dim in sides:
        count = lax.axis_size(axis)
        ends = count if closed else count - 1
        head = lax.slice_in_dim(cells, 0, width, axis=dim)
        tail = lax.slice_in_dim(cells, cells.shape[dim] - width, cells.shape[dim], axis=dim)
        cells = jnp.concatenate(
            [
                lax.ppermute(tail, axis, [(i, (i + 1) % count) for i in range(ends)]),
                cells,
                lax.ppermute(head, axis, [((i + 1) % count, i) for i in range(ends)]),
            ],
            axis=dim,
        )
    return cells


def fold_columns(extended, radius):
    inner_cols = extended.shape[2] - 2 * radius
    left_rim = extended[:, :, :radius]
    right_rim = extended[:, :, inner_cols + radius :]
    from_next = shifted(left_rim.astype(jnp.bfloat16), "lon", -1).astype(left_rim.dtype)
    from_prev = shifted(right_rim.astype(jnp.bfloat16), "lon", 1).astype(right_rim.dtype)
    central = extended[:, :, radius : inner_cols + radius]
    central = central.at[:, :, inner_cols - radius :].add(from_next)
    central = central.at[:, :, :radius].add(from_prev)
    return central


def fold_rows(extended, radius):
    inner_rows = extended.shape[1] - 2 * radius
    upper_rim = extended[:, :radius]
    lower_rim = extended[:, inner_rows + radius :]
    from_next = shifted_2(upper_rim.astype(jnp.bfloat16), "lat", -1).astype(upper_rim.dtype)
    from_prev = shifted_2(lower_rim.astype(jnp.bfloat16), "lat", 1).astype(lower_rim.dtype)
    central = extended[:, radius : inner_rows + radius]
    central = central.at[:, inner_rows - radius :].add(from_next)
    central = central.at[:, :radius].add(from_prev)
    return central


def on_device(queries, keys, values, grad_out, sink_logits):
    lat_rows, lon_cols, model_width = queries.shape
    head_count = sink_logits.shape[0]
    head_width = model_width // head_count
    radius = WIN // 2
    score_scale = head_width ** (-0.5)
    key_value = jnp.stack([keys, values])
    widened = extended_2(key_value, (("lat", 1),), radius, False)
    padded = extended_2(widened, (("lon", 2),), radius, True)
    band_rows = math.gcd(lat_rows, max(1, 512 // lon_cols))
    band_count = lat_rows // band_rows
    key_rows = band_rows + 2 * radius
    key_cols = lon_cols + 2 * radius
    query_row = jnp.repeat(jnp.arange(band_rows), lon_cols)
    query_col = jnp.tile(jnp.arange(lon_cols), band_rows)
    key_row = jnp.repeat(jnp.arange(key_rows), key_cols)
    key_col = jnp.tile(jnp.arange(key_cols), key_rows)
    row_offset = key_row[None, :] - query_row[:, None]
    col_offset = key_col[None, :] - query_col[:, None]
    local_mask = (
        (row_offset >= 0)
        & (row_offset <= 2 * radius)
        & (col_offset >= 0)
        & (col_offset <= 2 * radius)
    )
    first_row = lax.axis_index("lat") * lat_rows - radius
    total_rows = lat_rows * lax.axis_size("lat")
    sink_weight = jnp.exp(sink_logits - softcap)

    def band_mask(band_start):
        global_row = first_row + band_start + key_row
        return local_mask & ((global_row >= 0) & (global_row < total_rows))[None, :]

    def one_band(band_index, running):
        attended, query_grad, sink_local, grads_wide = running
        band_start = band_index * band_rows
        query_tile = queries.reshape(-1, model_width)
        grad_tile = grad_out.reshape(-1, model_width)
        key_tile = padded.reshape(2, -1, model_width)
        window_mask = band_mask(band_start)
        out_pieces = []
        query_pieces = []
        key_pieces = []
        value_pieces = []
        sink_pieces = []
        for head_index in range(head_count):
            head_start = head_index * head_width
            query_head = query_tile[:, head_start : head_start + head_width]
            grad_head = grad_tile[:, head_start : head_start + head_width]
            key_head = key_tile[0, :, head_start : head_start + head_width]
            value_head = key_tile[1, :, head_start : head_start + head_width]
            raw_scores = (
                jnp.dot(query_head, key_head.T, preferred_element_type=jnp.float32) * score_scale
            )
            squashed = jnp.tanh(raw_scores / softcap)
            weights = jnp.where(window_mask, jnp.exp(softcap * squashed - softcap), 0.0)
            denominator = jnp.sum(weights, axis=1) + sink_weight[head_index]
            attention = weights / denominator[:, None]
            attention_low = attention.astype(jnp.bfloat16)
            out_pieces.append(
                jnp.dot(attention_low, value_head, preferred_element_type=jnp.float32)
            )
            prob_grad = jnp.dot(grad_head, value_head.T, preferred_element_type=jnp.float32)
            delta_sum = jnp.sum(attention * prob_grad, axis=1)
            sink_pieces.append(-jnp.sum(sink_weight[head_index] / denominator * delta_sum))
            score_grad = (
                attention
                * (prob_grad - delta_sum[:, None])
                * (1.0 - squashed * squashed)
                * score_scale
            ).astype(jnp.bfloat16)
            query_pieces.append(jnp.dot(score_grad, key_head, preferred_element_type=jnp.float32))
            key_pieces.append(jnp.dot(score_grad.T, query_head, preferred_element_type=jnp.float32))
            value_pieces.append(
                jnp.dot(attention_low.T, grad_head, preferred_element_type=jnp.float32)
            )
        band_out = (
            jnp.concatenate(out_pieces, axis=1)
            .astype(jnp.bfloat16)
            .reshape(band_rows, lon_cols, model_width)
        )
        attended = band_out
        band_query = (
            jnp.concatenate(query_pieces, axis=1)
            .astype(jnp.bfloat16)
            .reshape(band_rows, lon_cols, model_width)
        )
        query_grad = band_query
        sink_local = sink_local + jnp.stack(sink_pieces)
        wide_part = jnp.stack(
            [jnp.concatenate(key_pieces, axis=1), jnp.concatenate(value_pieces, axis=1)]
        )
        wide_part = wide_part.reshape(2, key_rows, key_cols, model_width)
        current = grads_wide
        grads_wide = lax.dynamic_update_slice_in_dim(grads_wide, current + wide_part, band_start, 1)
        return (attended, query_grad, sink_local, grads_wide)

    initial = (
        jnp.zeros((lat_rows, lon_cols, model_width), jnp.bfloat16),
        jnp.zeros((lat_rows, lon_cols, model_width), jnp.bfloat16),
        jnp.zeros((head_count,), jnp.float32),
        jnp.zeros((2, lat_rows + 2 * radius, key_cols, model_width), jnp.float32),
    )
    attended, query_grad, sink_local, grads_wide = lax.fori_loop(0, band_count, one_band, initial)
    sink_grad = lax.psum(sink_local, ("lat", "lon"))
    folded = fold_rows(fold_columns(grads_wide, radius), radius)
    key_grad = folded[0].astype(jnp.bfloat16)
    value_grad = folded[1].astype(jnp.bfloat16)
    return (attended, query_grad, key_grad, value_grad, sink_grad)


def solution(mesh):
    return jax.shard_map(
        on_device,
        mesh=mesh,
        in_specs=(
            P("lat", "lon", None),
            P("lat", "lon", None),
            P("lat", "lon", None),
            P("lat", "lon", None),
            P(),
        ),
        out_specs=(
            P("lat", "lon", None),
            P("lat", "lon", None),
            P("lat", "lon", None),
            P("lat", "lon", None),
            P(),
        ),
        check_vma=False,
    )
```

profile of v0, /device:TPU:1, one launch (start us, length us, event | category | flops | bytes accessed | tf_op | source)
XLA Modules:
  0.0 304.0 jit_solution(6928717451433209931)
XLA Ops:
  3.3 4.6 %collective-permute-start = (bf16[2,6,32,512]{3,2,1,0:T(8,128)(2,1)S(1)}, bf16[2,6,32,512]{3,2,1,0:T(8,128)(2,1)S(1)}, u32[]{:S(2)}, u32[]{:S(2)}) collective-permute-start(bf16[2,6,32,512]{3,2,1,0:T(8,128)(2,1)S(1)} %get-tuple-element.146), channel_id=1, source_target_pairs={{0,32},{32,64},{64,96},{96,128},{128,160},{160,192},{192,224},{1,3... | collective-permute-start | bytes 1179656 | tf_op jit(solution)/shard_map/ppermute | solution.py:33
  8.6 3.9 %collective-permute-done.1 = bf16[2,6,32,512]{3,2,1,0:T(8,128)(2,1)S(1)} collective-permute-done((bf16[2,6,32,512]{3,2,1,0:T(8,128)(2,1)S(1)}, bf16[2,6,32,512]{3,2,1,0:T(8,128)(2,1)S(1)}, u32[]{:S(2)}, u32[]{:S(2)}) %collective-permute-start.1) | collective-permute-done | bytes 393248 | tf_op jit(solution)/shard_map/ppermute | solution.py:35
  14.4 3.9 %collective-permute-start.3 = (bf16[2,20,6,512]{3,2,1,0:T(8,128)(2,1)S(1)}, bf16[2,20,6,512]{3,2,1,0:T(8,128)(2,1)S(1)}, u32[]{:S(2)}, u32[]{:S(2)}) collective-permute-start(bf16[2,20,6,512]{3,2,1,0:T(8,128)(2,1)S(1)} %get-tuple-element.127), channel_id=1, source_target_pairs={{1,0},{2,1},{3,2},{4,3},{5,4},{6,5},{7,6},{8,7},{9,8},{10,9},{11,1... | collective-permute-start | bytes 737288 | tf_op jit(solution)/shard_map/ppermute | solution.py:35
  18.3 1.9 collective-permute-start.2
  22.9 1.9 collective-permute-done.3
  27.5 1.9 copy.29
  29.4 8.0 %fusion.128 = (bf16[1,880,64]{2,0,1:T(2,128)(2,1)}, bf16[1,880,64]{2,0,1:T(2,128)(2,1)}, bf16[1,880,64]{2,0,1:T(2,128)(2,1)S(1)}, bf16[1,880,64]{2,0,1:T(2,128)(...) fusion(bf16[2,880,512]{2,0,1:T(2,128)(2,1)S(1)} %bitcast.337), kind=kLoop, calls=%fused_computation.238 | loop fusion | bytes 3604480 | tf_op jit(solution)/shard_map/while/body/eval_jaxpr/slice | solution.py:116
  38.7 1.9 copy.67
  54.7 2.0 copy.65
  56.7 2.2 convolution_bitcast_fusion.6
  58.9 2.1 convolution_bitcast_fusion.7
  63.1 2.4 fusion.45
  66.9 4.8 %multiply_reduce_fusion = (f32[256]{0:T(256)}, f32[256]{0:T(256)S(1)}, f32[256]{0:T(256)S(1)}, f32[256]{0:T(256)}, f32[256]{0:T(256)}, /*index=5*/f32[256]{0:T(2...) fusion(f32[256]{0:T(256)S(1)} %broadcast_add_fusion, f32[880,256]{1,0:T(8,128)S(1)} %get-tuple-element.166, ...), kind=kOutput, calls=%fused_computation.93 | convolution fusion | flops 39196672 | bytes 9212928 | tf_op jit(solution)/shard_map/while/body/eval_jaxpr/dot_general | solution.py:128
  73.1 2.2 multiply_reduce_fusion.5
  92.8 1.9 fusion.112
  97.4 4.5 %multiply_reduce_fusion.1 = (f32[256]{0:T(256)S(1)}, f32[256]{0:T(256)S(1)}, f32[256]{0:T(256)S(1)}, f32[256]{0:T(256)S(1)}, f32[256,880]{0,1:T(8,128)}) fusion(f32[256]{0:T(256)S(1)} %broadcast_add_fusion.1, f32[880,256]{1,0:T(8,128)S(1)} %copy-done.16, pred[880]{0:T(1024)(128)(4,1)S(1)} %copy-done.66, s32[256]{0:T(256)S(1)} %copy-done.60, ...), kind=kOutput, calls=%fused_computation.94 | convolution fusion | flops 36494336 | bytes 7406592 | tf_op jit(solution)/shard_map/while/body/eval_jaxpr/dot_general | solution.py:128
  103.8 2.8 fusion.15
  107.0 1.9 convolution_convert_fusion.13
  112.1 2.7 fusion.111
  114.8 4.5 %fusion.9 = (bf16[256,880]{0,1:T(8,128)(2,1)S(1)}, bf16[256,880]{0,1:T(8,128)(2,1)}, bf16[256,880]{0,1:T(8,128)(2,1)}, bf16[256,880]{0,1:T(8,128)(2,1)S(1)}, bf1...) fusion(f32[880,256]{1,0:T(8,128)} %copy-done.49, f32[256,880]{0,1:T(8,128)} %get-tuple-element.167, ...), kind=kLoop, calls=%fused_computation.63 | loop fusion | flops 10362880 | bytes 8126192 | tf_op jit(solution)/shard_map/while/body/eval_jaxpr/convert_element_type | solution.py:136
  119.3 2.3 copy.46
  121.7 1.9 convolution_convert_fusion.10
  123.6 2.0 copy.49
  125.6 2.0 convolution_convert_fusion.9
  127.5 2.0 copy.52
  129.5 1.9 convolution_convert_fusion.8
  131.5 1.9 convolution_convert_fusion.7
  134.4 1.9 convolution_convert_fusion.6
  136.3 2.0 copy.56
  138.3 1.9 convolution_convert_fusion.5
  140.3 2.0 copy.57
  142.2 1.9 convolution_convert_fusion.4
  145.2 2.0 convolution_convert_fusion.3
  147.1 1.9 convolution_dynamic-update-slice_fusion.14
  149.0 2.0 convolution_dynamic-update-slice_fusion.13
  151.0 1.9 convolution_dynamic-update-slice_fusion.12
  156.9 2.7 copy.62
  169.9 2.8 copy.63
  175.7 2.5 convert.76
  179.1 9.0 %collective-permute-start.4 = (bf16[2,20,6,512]{3,2,1,0:T(8,128)(2,1)}, bf16[2,20,6,512]{3,2,1,0:T(8,128)(2,1)}, u32[]{:S(2)}, u32[]{:S(2)}) collective-permute-start(bf16[2,20,6,512]{3,2,1,0:T(8,128)(2,1)} %get-tuple-element.107), channel_id=1, source_target_pairs={{0,31},{1,0},{2,1},{3,2},{4,3},{5,4},{6,5},{7,6},{8,7},{9,8},{10,9... | collective-permute-start | bytes 737288 | tf_op jit(solution)/shard_map/ppermute | solution.py:16
  188.1 1.9 fusion.116
  192.9 2.5 slice.418
  203.4 2.1 scatter-add.14
  206.5 2.3 scatter-add.15
  212.1 4.8 %collective-permute-start.7 = (bf16[2,6,32,512]{3,2,1,0:T(8,128)(2,1)S(1)}, bf16[2,6,32,512]{3,2,1,0:T(8,128)(2,1)S(1)}, u32[]{:S(2)}, u32[]{:S(2)}) collective-permute-start(bf16[2,6,32,512]{3,2,1,0:T(8,128)(2,1)S(1)} %get-tuple-element.124), channel_id=1, source_target_pairs={{0,32},{32,64},{64,96},{96,128},{128,160},{160,192},{192,224},{1,3... | collective-permute-start | bytes 1179656 | tf_op jit(solution)/shard_map/ppermute | solution.py:22
  217.8 79.9 %psum.7 = f32[8]{0:T(128)} all-reduce(f32[8]{0:T(128)S(1)} %copy-done.93), channel_id=1, replica_groups=mesh['lat'=8,'lon'=32] {'lat','lon'}, use_global_device_ids=true, to_apply=%region_24.0 | all-reduce | flops 8 | bytes 64 | tf_op jit(solution)/shard_map/psum | solution.py:170
  297.7 1.9 concatenate.37
  299.7 1.9 concatenate.38
  (291 shorter events, 89.2 us)
Async XLA Ops:
  0.6 25.8 %copy-start.31 = (bf16[8,32,512]{2,1,0:T(8,128)(2,1)S(1)}, bf16[8,32,512]{2,1,0:T(8,128)(2,1)}, u32[]{:S(2)}) copy-start(bf16[8,32,512]{2,1,0:T(8,128)(2,1)} %param.14) | copy-start | bytes 786436
  0.6 25.8 %copy-start.32 = (bf16[8,32,512]{2,1,0:T(8,128)(2,1)S(1)}, bf16[8,32,512]{2,1,0:T(8,128)(2,1)}, u32[]{:S(2)}) copy-start(bf16[8,32,512]{2,1,0:T(8,128)(2,1)} %param.15) | copy-start | bytes 786436
  2.0 10.4 %collective-permute-start.1 = (bf16[2,6,32,512]{3,2,1,0:T(8,128)(2,1)S(1)}, bf16[2,6,32,512]{3,2,1,0:T(8,128)(2,1)S(1)}, u32[]{:S(2)}, u32[]{:S(2)}) collective-permute-start(bf16[2,6,32,512]{3,2,1,0:T(8,128)(2,1)S(1)} %get-tuple-element.147), channel_id=1, source_target_pairs={{32,0},{64,32},{96,64},{128,96},{160,128},{192,160},{224,192},{33,... | collective-permute-start | bytes 1179656 | tf_op jit(solution)/shard_map/ppermute | solution.py:35
  3.3 10.0 %collective-permute-start = (bf16[2,6,32,512]{3,2,1,0:T(8,128)(2,1)S(1)}, bf16[2,6,32,512]{3,2,1,0:T(8,128)(2,1)S(1)}, u32[]{:S(2)}, u32[]{:S(2)}) collective-permute-start(bf16[2,6,32,512]{3,2,1,0:T(8,128)(2,1)S(1)} %get-tuple-element.146), channel_id=1, source_target_pairs={{0,32},{32,64},{64,96},{96,128},{128,160},{160,192},{192,224},{1,3... | collective-permute-start | bytes 1179656 | tf_op jit(solution)/shard_map/ppermute | solution.py:33
  14.4 10.5 %collective-permute-start.3 = (bf16[2,20,6,512]{3,2,1,0:T(8,128)(2,1)S(1)}, bf16[2,20,6,512]{3,2,1,0:T(8,128)(2,1)S(1)}, u32[]{:S(2)}, u32[]{:S(2)}) collective-permute-start(bf16[2,20,6,512]{3,2,1,0:T(8,128)(2,1)S(1)} %get-tuple-element.127), channel_id=1, source_target_pairs={{1,0},{2,1},{3,2},{4,3},{5,4},{6,5},{7,6},{8,7},{9,8},{10,9},{11,1... | collective-permute-start | bytes 737288 | tf_op jit(solution)/shard_map/ppermute | solution.py:35
  18.3 8.1 %collective-permute-start.2 = (bf16[2,20,6,512]{3,2,1,0:T(8,128)(2,1)S(1)}, bf16[2,20,6,512]{3,2,1,0:T(8,128)(2,1)S(1)}, u32[]{:S(2)}, u32[]{:S(2)}) collective-permute-start(bf16[2,20,6,512]{3,2,1,0:T(8,128)(2,1)S(1)} %get-tuple-element.126), channel_id=1, source_target_pairs={{0,1},{1,2},{2,3},{3,4},{4,5},{5,6},{6,7},{7,8},{8,9},{9,10},{10,1... | collective-permute-start | bytes 737288 | tf_op jit(solution)/shard_map/ppermute | solution.py:33
  20.9 82.9 %copy-start.54 = (s32[880]{0:T(1024)}, s32[880]{0:T(1024)S(1)}, u32[]{:S(2)}) copy-start(s32[880]{0:T(1024)S(1)} %sub.242) | copy-start | bytes 10564
  21.7 82.1 %copy-start.56 = (s32[880]{0:T(1024)}, s32[880]{0:T(1024)S(1)}, u32[]{:S(2)}) copy-start(s32[880]{0:T(1024)S(1)} %sub.247) | copy-start | bytes 10564
  29.4 12.4 %copy-start.12 = (bf16[8,32,512]{2,1,0:T(8,128)(2,1)S(1)}, bf16[8,32,512]{2,1,0:T(8,128)(2,1)}, u32[]{:S(2)}) copy-start(bf16[8,32,512]{2,1,0:T(8,128)(2,1)} %param.13) | copy-start | bytes 786436
  53.6 43.6 %copy-start.14 = (f32[880,256]{1,0:T(8,128)}, f32[880,256]{1,0:T(8,128)S(1)}, u32[]{:S(2)}) copy-start(f32[880,256]{1,0:T(8,128)S(1)} %fusion.2) | copy-start | bytes 2703364
  54.6 12.2 %copy-start.15 = (f32[880,256]{1,0:T(8,128)}, f32[880,256]{1,0:T(8,128)S(1)}, u32[]{:S(2)}) copy-start(f32[880,256]{1,0:T(8,128)S(1)} %fusion.1) | copy-start | bytes 2703364
  54.6 8.4 %copy-start.58 = (s32[256]{0:T(256)S(1)}, s32[256]{0:T(256)}, u32[]{:S(2)}) copy-start(s32[256]{0:T(256)} %sub.249) | copy-start | bytes 3076
  54.6 8.4 %copy-start.61 = (s32[256]{0:T(256)S(1)}, s32[256]{0:T(256)}, u32[]{:S(2)}) copy-start(s32[256]{0:T(256)} %sub.244) | copy-start | bytes 3076
  54.7 8.4 %copy-start.64 = (pred[880]{0:T(1024)(128)(4,1)S(1)}, pred[880]{0:T(1024)(128)(4,1)}, u32[]{:S(2)}) copy-start(pred[880]{0:T(1024)(128)(4,1)} %compare_and_fusion) | copy-start | bytes 2644
  63.1 10.0 %copy-start.53 = (bf16[1,880,64]{1,2,0:T(8,128)(2,1)}, bf16[1,880,64]{1,2,0:T(8,128)(2,1)S(1)}, u32[]{:S(2)}) copy-start(bf16[1,880,64]{1,2,0:T(8,128)(2,1)S(1)} %copy.69) | copy-start | bytes 337924
  85.7 9.0 %copy-start.83 = (f32[256]{0:T(256)S(1)}, f32[256]{0:T(256)}, u32[]{:S(2)}) copy-start(f32[256]{0:T(256)} %get-tuple-element.96) | copy-start | bytes 3076
  85.7 9.7 %copy-start.81 = (f32[256]{0:T(256)S(1)}, f32[256]{0:T(256)}, u32[]{:S(2)}) copy-start(f32[256]{0:T(256)} %get-tuple-element.95) | copy-start | bytes 3076
  85.7 10.3 %copy-start.88 = (f32[256]{0:T(256)S(1)}, f32[256]{0:T(256)}, u32[]{:S(2)}) copy-start(f32[256]{0:T(256)} %get-tuple-element.94) | copy-start | bytes 3076
  85.8 10.9 %copy-start.87 = (f32[256]{0:T(256)S(1)}, f32[256]{0:T(256)}, u32[]{:S(2)}) copy-start(f32[256]{0:T(256)} %get-tuple-element.93) | copy-start | bytes 3076
  85.8 11.5 %copy-start.16 = (f32[880,256]{1,0:T(8,128)S(1)}, f32[880,256]{1,0:T(8,128)}, u32[]{:S(2)}) copy-start(f32[880,256]{1,0:T(8,128)} %copy-done.15) | copy-start | bytes 2703364
  85.8 11.5 %copy-start.60 = (s32[256]{0:T(256)S(1)}, s32[256]{0:T(256)}, u32[]{:S(2)}) copy-start(s32[256]{0:T(256)} %sub.249) | copy-start | bytes 3076
  85.8 11.5 %copy-start.63 = (s32[256]{0:T(256)S(1)}, s32[256]{0:T(256)}, u32[]{:S(2)}) copy-start(s32[256]{0:T(256)} %sub.244) | copy-start | bytes 3076
  85.8 11.5 %copy-start.66 = (pred[880]{0:T(1024)(128)(4,1)S(1)}, pred[880]{0:T(1024)(128)(4,1)}, u32[]{:S(2)}) copy-start(pred[880]{0:T(1024)(128)(4,1)} %compare_and_fusion) | copy-start | bytes 2644
  87.2 14.7 %copy-start.43 = (bf16[1,880,64]{1,2,0:T(8,128)(2,1)}, bf16[1,880,64]{1,2,0:T(8,128)(2,1)S(1)}, u32[]{:S(2)}) copy-start(bf16[1,880,64]{1,2,0:T(8,128)(2,1)S(1)} %copy.75) | copy-start | bytes 337924
  89.7 12.2 %copy-start.48 = (bf16[1,880,64]{1,2,0:T(8,128)(2,1)}, bf16[1,880,64]{1,2,0:T(8,128)(2,1)S(1)}, u32[]{:S(2)}) copy-start(bf16[1,880,64]{1,2,0:T(8,128)(2,1)S(1)} %copy.71) | copy-start | bytes 337924
  101.9 12.9 %copy-start.71 = (f32[256]{0:T(256)}, f32[256]{0:T(256)S(1)}, u32[]{:S(2)}) copy-start(f32[256]{0:T(256)S(1)} %get-tuple-element.98) | copy-start | bytes 3076
  101.9 12.8 %copy-start.73 = (f32[256]{0:T(256)}, f32[256]{0:T(256)S(1)}, u32[]{:S(2)}) copy-start(f32[256]{0:T(256)S(1)} %get-tuple-element.99) | copy-start | bytes 3076
  106.9 7.8 %copy-start.55 = (s32[880]{0:T(1024)S(1)}, s32[880]{0:T(1024)}, u32[]{:S(2)}) copy-start(s32[880]{0:T(1024)} %copy-done.54) | copy-start | bytes 10564
  106.9 7.8 %copy-start.57 = (s32[880]{0:T(1024)S(1)}, s32[880]{0:T(1024)}, u32[]{:S(2)}) copy-start(s32[880]{0:T(1024)} %copy-done.56) | copy-start | bytes 10564
  106.9 7.8 %copy-start.68 = (f32[256]{0:T(256)S(1)}, f32[256]{0:T(256)}, u32[]{:S(2)}) copy-start(f32[256]{0:T(256)} %copy-done.67) | copy-start | bytes 3076
  119.3 34.5 %copy-start.4 = (bf16[256,880]{0,1:T(8,128)(2,1)}, bf16[256,880]{0,1:T(8,128)(2,1)S(1)}, u32[]{:S(2)}) copy-start(bf16[256,880]{0,1:T(8,128)(2,1)S(1)} %get-tuple-element.151) | copy-start | bytes 1351684
  119.3 35.5 %copy-start = (bf16[256,880]{0,1:T(8,128)(2,1)}, bf16[256,880]{0,1:T(8,128)(2,1)S(1)}, u32[]{:S(2)}) copy-start(bf16[256,880]{0,1:T(8,128)(2,1)S(1)} %get-tuple-element.149) | copy-start | bytes 1351684
  125.6 8.8 %copy-start.37 = (bf16[1,880,64]{1,2,0:T(8,128)(2,1)S(1)}, bf16[1,880,64]{1,2,0:T(8,128)(2,1)}, u32[]{:S(2)}) copy-start(bf16[1,880,64]{1,2,0:T(8,128)(2,1)} %copy-done.36) | copy-start | bytes 337924
  136.3 8.9 %copy-start.39 = (bf16[1,880,64]{1,2,0:T(8,128)(2,1)S(1)}, bf16[1,880,64]{1,2,0:T(8,128)(2,1)}, u32[]{:S(2)}) copy-start(bf16[1,880,64]{1,2,0:T(8,128)(2,1)} %copy-done.38) | copy-start | bytes 337924
  175.7 12.4 %copy-start.72 = (f32[256]{0:T(256)S(1)}, f32[256]{0:T(256)}, u32[]{:S(2)}) copy-start(f32[256]{0:T(256)} %copy-done.71) | copy-start | bytes 3076
  175.7 12.4 %copy-start.74 = (f32[256]{0:T(256)S(1)}, f32[256]{0:T(256)}, u32[]{:S(2)}) copy-start(f32[256]{0:T(256)} %copy-done.73) | copy-start | bytes 3076
  175.7 12.4 %copy-start.82 = (f32[256]{0:T(256)S(1)}, f32[256]{0:T(256)}, u32[]{:S(2)}) copy-start(f32[256]{0:T(256)} %get-tuple-element.95) | copy-start | bytes 3076
  175.7 12.4 %copy-start.84 = (f32[256]{0:T(256)S(1)}, f32[256]{0:T(256)}, u32[]{:S(2)}) copy-start(f32[256]{0:T(256)} %get-tuple-element.96) | copy-start | bytes 3076
  175.7 14.3 %copy-start.5 = (bf16[256,880]{0,1:T(8,128)(2,1)S(1)}, bf16[256,880]{0,1:T(8,128)(2,1)}, u32[]{:S(2)}) copy-start(bf16[256,880]{0,1:T(8,128)(2,1)} %copy-done.4) | copy-start | bytes 1351684
  178.2 12.8 %copy-start.1 = (bf16[256,880]{0,1:T(8,128)(2,1)S(1)}, bf16[256,880]{0,1:T(8,128)(2,1)}, u32[]{:S(2)}) copy-start(bf16[256,880]{0,1:T(8,128)(2,1)} %copy-done) | copy-start | bytes 1351684
  179.1 23.0 %collective-permute-start.4 = (bf16[2,20,6,512]{3,2,1,0:T(8,128)(2,1)}, bf16[2,20,6,512]{3,2,1,0:T(8,128)(2,1)}, u32[]{:S(2)}, u32[]{:S(2)}) collective-permute-start(bf16[2,20,6,512]{3,2,1,0:T(8,128)(2,1)} %get-tuple-element.107), channel_id=1, source_target_pairs={{0,31},{1,0},{2,1},{3,2},{4,3},{5,4},{6,5},{7,6},{8,7},{9,8},{10,9... | collective-permute-start | bytes 737288 | tf_op jit(solution)/shard_map/ppermute | solution.py:16
  192.9 8.3 %copy-start.35 = (bf16[256,880]{1,0:T(8,128)(2,1)S(1)}, bf16[256,880]{1,0:T(8,128)(2,1)}, u32[]{:S(2)}) copy-start(bf16[256,880]{1,0:T(8,128)(2,1)} %copy.59) | copy-start | bytes 1351684
  195.4 10.1 %collective-permute-start.5 = (bf16[2,20,6,512]{3,2,1,0:T(8,128)(2,1)}, bf16[2,20,6,512]{3,2,1,0:T(8,128)(2,1)}, u32[]{:S(2)}, u32[]{:S(2)}) collective-permute-start(bf16[2,20,6,512]{3,2,1,0:T(8,128)(2,1)} %get-tuple-element.106), channel_id=1, source_target_pairs={{0,1},{1,2},{2,3},{3,4},{4,5},{5,6},{6,7},{7,8},{8,9},{9,10},{10,1... | collective-permute-start | bytes 737288 | tf_op jit(solution)/shard_map/ppermute | solution.py:16
  209.0 7.8 %copy-start.33 = (bf16[256,880]{1,0:T(8,128)(2,1)S(1)}, bf16[256,880]{1,0:T(8,128)(2,1)}, u32[]{:S(2)}) copy-start(bf16[256,880]{1,0:T(8,128)(2,1)} %copy.61) | copy-start | bytes 1351684
  209.1 7.8 %copy-start.51 = (bf16[1,880,64]{1,2,0:T(8,128)(2,1)S(1)}, bf16[1,880,64]{1,2,0:T(8,128)(2,1)}, u32[]{:S(2)}) copy-start(bf16[1,880,64]{1,2,0:T(8,128)(2,1)} %copy.78) | copy-start | bytes 337924
  209.1 8.7 %copy-start.93 = (f32[8]{0:T(128)S(1)}, f32[8]{0:T(128)}, u32[]{:S(2)}) copy-start(f32[8]{0:T(128)} %stack.71) | copy-start | bytes 100
  209.9 91.8 %collective-permute-start.6 = (bf16[2,6,32,512]{3,2,1,0:T(8,128)(2,1)}, bf16[2,6,32,512]{3,2,1,0:T(8,128)(2,1)}, u32[]{:S(2)}, u32[]{:S(2)}) collective-permute-start(bf16[2,6,32,512]{3,2,1,0:T(8,128)(2,1)} %get-tuple-element.125), channel_id=1, source_target_pairs={{32,0},{64,32},{96,64},{128,96},{160,128},{192,160},{224,192},{33,... | collective-permute-start | bytes 1179656 | tf_op jit(solution)/shard_map/ppermute | solution.py:22
  212.1 90.8 %collective-permute-start.7 = (bf16[2,6,32,512]{3,2,1,0:T(8,128)(2,1)S(1)}, bf16[2,6,32,512]{3,2,1,0:T(8,128)(2,1)S(1)}, u32[]{:S(2)}, u32[]{:S(2)}) collective-permute-start(bf16[2,6,32,512]{3,2,1,0:T(8,128)(2,1)S(1)} %get-tuple-element.124), channel_id=1, source_target_pairs={{0,32},{32,64},{64,96},{96,128},{128,160},{160,192},{192,224},{1,3... | collective-permute-start | bytes 1179656 | tf_op jit(solution)/shard_map/ppermute | solution.py:22
  (54 other events, 247.2 us)
where the time goes:
time: 306 us; the launch traced here: 304 us
  blocking collectives  79.9 us (26%)
  local copies, waits for them, and re-layouts  75.2 us (25%)
  matrix products  73.4 us (24%)
  other arithmetic  33.4 us (11%)
  starting transfers between devices  26.8 us (9%)
  waiting for transfers between devices  8.27 us (3%)
  between operations  7.11 us (2%)
    psum x1, blocking collectives, on_device(): sink_grad = lax.psum(sink_local, ('lat', 'lon'))  79.9 us
    unnamed x205, local copies, waits for them, and re-layouts  21.7 us
    dot_general x8, matrix products, one_band(): jnp.dot(grad_head, value_head.T, preferred_element_type=jnp.float32)  19.7 us
    dot_general x8, matrix products, one_band(): jnp.dot(attention_low, value_head, preferred_element_type=jnp.float32)  13.1 us
    dot_general x8, matrix products, one_band(): jnp.dot(score_grad, key_head, preferred_element_type=jnp.float32)  12.4 us
    dot_general x8, matrix products, one_band(): jnp.dot(score_grad.T, query_head, preferred_element_type=jnp.float32)  10.7 us
    convert_element_type x8, local copies, waits for them, and re-layouts, one_band(): score_grad = (attention * (prob_grad - delta_sum[:, None]) * (1.0 - squas...  9.93 us
    dot_general x8, matrix products, one_band(): jnp.dot(query_head, key_head.T, preferred_element_type=jnp.float32)  9.44 us
  transfers between devices with their start and end apart: 8, of which 4 were waited for; matrix products, arithmetic and copies ran while one was open for 7% of the time, Pallas kernels for 0%

commit v1 on v0

v1 whole, which is shorter than its diff:
```python
import functools
import math

import jax
import jax.numpy as jnp
from jax import lax
from jax.experimental import pallas as pl
from jax.experimental.pallas import tpu as pltpu
from jax.sharding import PartitionSpec as P

WIN = 13
RADIUS = WIN // 2
SOFTCAP = 8.0
PAIRS = 4
ROWS = 8
COLS = 32
WIDE = 8
EXT_ROWS = ROWS + 2 * RADIUS
EXT_COLS = COLS + 2 * WIDE
TILE = 16
SPAN = TILE + 2 * WIDE
CHUNK = 4
N_CHUNK = EXT_ROWS // CHUNK
KEYS = CHUNK * SPAN
QN = ROWS * TILE
LANES = 128
N_LAT = 8
N_LON = 32
N_Z = 8
MESH = pl.DeviceIdType.MESH
BF16 = jnp.bfloat16
F32 = jnp.float32
EXP2_RATE = SOFTCAP * math.log2(math.e)

NT = (((1,), (1,)), ((), ()))
TN = (((0,), (0,)), ((), ()))


def dot(a, b, dims=(((1,), (0,)), ((), ()))):
    return lax.dot_general(a, b, dims, preferred_element_type=F32)


def head_blocks(turned):
    first = lax.broadcasted_iota(jnp.int32, (LANES, QN), 0) < LANES // 2
    return jnp.concatenate(
        [jnp.where(first, turned, 0.0), jnp.where(first, 0.0, turned)], axis=1
    )


def own_heads(both):
    first = lax.broadcasted_iota(jnp.int32, (LANES, QN), 0) < LANES // 2
    return jnp.where(first, both[:, :QN], both[:, QN:])


def kernel(
    q_hbm, k_hbm, v_hbm, g_hbm, sink_ref,
    o_hbm, dq_hbm, dk_hbm, dv_hbm, sg_ref,
    q_s, kv_s, g_s, ext, top, bot, mask,
    strip_to, strip_from, gstrip_to, gstrip_from, rim_to, rim_from,
    acc, e_s, u_s, out_s, sk, sk_all,
    in_sem, out_sem, lat_send, lat_recv, strip_send, strip_recv,
    gs_send, gs_recv, rim_send, rim_recv, sk_send, sk_recv, entered, met,
):
    a = lax.axis_index("lat")
    b = lax.axis_index("lon")
    up = (lax.rem(a + N_LAT - 1, N_LAT), b)
    down = (lax.rem(a + 1, N_LAT), b)
    left = (a, lax.rem(b + N_LON - 1, N_LON))
    right = (a, lax.rem(b + 1, N_LON))
    sides = (left, right)
    column = lax.rem(b, 2 * N_Z)
    z = column // 2
    is_first = column == 0
    is_last = column == 2 * N_Z - 1

    def lat_peer(d):
        return (lax.rem(a + d, N_LAT), b)

    def quad_peer(d):
        other = lax.rem(lax.rem(b, 2) + 2 * (b // (2 * N_Z)) + d, 4)
        return (a, lax.rem(other, 2) + 2 * z + 2 * N_Z * (other // 2))

    def z_peer(d):
        return (a, lax.rem(b, 2) + 2 * lax.rem(z + d, N_Z) + 2 * N_Z * (b // (2 * N_Z)))

    def load(i, p):
        src = (q_hbm, k_hbm, v_hbm, g_hbm)[i]
        dst = (q_s, kv_s.at[0], kv_s.at[1], g_s)[i]
        return pltpu.make_async_copy(
            src.at[:, :, pl.ds(pl.multiple_of(p * LANES, LANES), LANES)], dst.at[p], in_sem.at[i, p]
        )

    for p in range(PAIRS):
        for i in (1, 2):
            load(i, p).start()
    for p in range(PAIRS):
        for i in (0, 3):
            load(i, p).start()

    barrier = pltpu.get_barrier_semaphore()

    def greet(device):
        pl.semaphore_signal(barrier, inc=1, device_id=device, device_id_type=MESH)

    for d in range(1, N_LAT):
        greet(lat_peer(d))
    for d in range(1, 4):
        greet(quad_peer(d))
    @pl.when(jnp.logical_not(is_last))
    def _():
        greet(right)

    @pl.when(is_first)
    def _():
        greet(left)

    for d in range(1, N_Z):
        @pl.when(z + d < N_Z)
        def _():
            greet(z_peer(d))

    expect = N_LAT - 1 + 3 + z + jnp.where(is_first, 0, 1) + jnp.where(is_last, 1, 0)
    pl.semaphore_wait(barrier, expect)

    def lat_copy(p, i, side):
        src = (k_hbm, v_hbm)[i]
        first_row = (0, ROWS - RADIUS)[side]
        return pltpu.make_async_remote_copy(
            src_ref=src.at[
                first_row : first_row + RADIUS, :, pl.ds(pl.multiple_of(p * LANES, LANES), LANES)
            ],
            dst_ref=(bot, top)[side].at[p, i],
            send_sem=lat_send.at[p, i, side],
            recv_sem=lat_recv.at[p, i, side],
            device_id=(up, down)[side],
            device_id_type=MESH,
        )

    for p in range(PAIRS):
        for i in range(2):
            for side in range(2):
                lat_copy(p, i, side).start()

    @pl.when(jnp.logical_not(is_first))
    def _():
        pl.semaphore_signal(entered.at[1], inc=1, device_id=left, device_id_type=MESH)

    @pl.when(is_last)
    def _():
        pl.semaphore_signal(entered.at[0], inc=1, device_id=right, device_id_type=MESH)

    for d in range(1, N_Z):
        @pl.when(z - d >= 0)
        def _():
            pl.semaphore_signal(met, inc=1, device_id=z_peer(N_Z - d), device_id_type=MESH)

    key = lax.broadcasted_iota(jnp.int32, (EXT_ROWS * SPAN, QN), 0)
    query = lax.broadcasted_iota(jnp.int32, (EXT_ROWS * SPAN, QN), 1)
    key_row = key // SPAN - RADIUS
    row_gap = key_row - query // TILE
    col_gap = lax.rem(key, SPAN) - WIDE - lax.rem(query, TILE)
    whole_row = a * ROWS + key_row
    meets = (
        (row_gap >= -RADIUS) & (row_gap <= RADIUS) & (col_gap >= -RADIUS) & (col_gap <= RADIUS)
        & (whole_row >= 0) & (whole_row < N_LAT * ROWS)
    )
    mask[...] = jnp.where(meets, 1.0, 0.0)

    def rows_of(p, i, r):
        if r < RADIUS:
            return top[p, i, r].astype(F32)
        if r < RADIUS + ROWS:
            return kv_s[i, p, r - RADIUS].astype(F32)
        return bot[p, i, r - RADIUS - ROWS].astype(F32)

    def pack(p, first, last):
        for rp in range(first, last):
            for i in range(2):
                upper, lower = rows_of(p, i, 2 * rp), rows_of(p, i, 2 * rp + 1)
                strip_to[p, 0, rp, i] = jnp.concatenate([upper[:WIDE], lower[:WIDE]], 0).astype(BF16)
                strip_to[p, 1, rp, i] = jnp.concatenate(
                    [upper[COLS - WIDE :], lower[COLS - WIDE :]], 0
                ).astype(BF16)

    spans = ((3, 4), (0, 3), (7, 3))

    def strip_copy(p, side, part):
        first, count = spans[part]
        return pltpu.make_async_remote_copy(
            src_ref=strip_to.at[p, side, first : first + count],
            dst_ref=strip_from.at[p, 1 - side, first : first + count],
            send_sem=strip_send.at[p, side, part],
            recv_sem=strip_recv.at[p, 1 - side, part],
            device_id=sides[side],
            device_id_type=MESH,
        )

    for p in range(PAIRS):
        for i in (1, 2):
            load(i, p).wait()
        pack(p, 3, 7)

    @pl.when(jnp.logical_not(is_last))
    def _():
        pl.semaphore_wait(entered.at[1], 1)

    @pl.when(is_first)
    def _():
        pl.semaphore_wait(entered.at[0], 1)

    for p in range(PAIRS):
        for side in range(2):
            strip_copy(p, side, 0).start()

    acc[...] = jnp.zeros_like(acc)

    def stage_a(p):
        for i in range(2):
            for side in range(2):
                lat_copy(p, i, side).wait_recv()
        pack(p, 0, 3)
        pack(p, 7, 10)
        for side in range(2):
            for part in (1, 2):
                strip_copy(p, side, part).start()

    def stage_ext(p):
        for side in range(2):
            for part in range(3):
                strip_copy(p, side, part).wait_recv()
        for rp in range(EXT_ROWS // 2):
            for i in range(2):
                west = strip_from[p, 0, rp, i].astype(F32)
                east = strip_from[p, 1, rp, i].astype(F32)
                for j in range(2):
                    half = slice(j * WIDE, (j + 1) * WIDE)
                    ext[i, 2 * rp + j] = jnp.concatenate(
                        [west[half], rows_of(p, i, 2 * rp + j), east[half]], 0
                    ).astype(BF16)

    def attend(p, tile):
        at = pl.multiple_of(tile * TILE, TILE)
        cols = pl.ds(at, TILE)
        span = pl.ds(at, SPAN)
        q_turned = q_s[p, :, cols, :].reshape(QN, LANES).astype(F32).T
        g_turned = g_s[p, :, cols, :].reshape(QN, LANES).astype(F32).T
        q_blocks = head_blocks(q_turned)
        g_blocks = head_blocks(g_turned)
        q_low = (q_blocks * (1.0 / 64.0)).astype(BF16)
        g_low = g_blocks.astype(BF16)
        lane = lax.broadcasted_iota(jnp.int32, (1, 2 * QN), 1)
        sink = jnp.exp(jnp.where(lane < QN, sink_ref[2 * p], sink_ref[2 * p + 1]))
        total = jnp.zeros((8, 2 * QN), F32)
        out = jnp.zeros((LANES, 2 * QN), F32)
        for c in range(N_CHUNK):
            here = slice(c * KEYS, (c + 1) * KEYS)
            k_here = ext[0, c * CHUNK : (c + 1) * CHUNK, span, :].reshape(KEYS, LANES)
            v_here = ext[1, c * CHUNK : (c + 1) * CHUNK, span, :].reshape(KEYS, LANES)
            squashed = jnp.tanh(dot(k_here, q_low))
            meets_here = mask[here, :]
            weight = jnp.exp2(squashed * EXP2_RATE) * jnp.concatenate([meets_here, meets_here], 1)
            total = total + jnp.sum(weight.reshape(KEYS // 8, 8, 2 * QN), axis=0)
            weight_low = weight.astype(BF16)
            e_s[here, :] = weight_low
            u_s[here, :] = (weight * (1.0 - squashed * squashed)).astype(BF16)
            out = out + dot(v_here, weight_low, TN)
        inverse = 1.0 / (jnp.sum(total, axis=0, keepdims=True) + sink)
        out = out * inverse
        delta = jnp.sum(g_blocks * out, axis=0, keepdims=True)
        out_s[0, p, :, cols, :] = own_heads(out).T.reshape(ROWS, TILE, LANES).astype(BF16)
        share = sink * inverse * delta
        sk[p, :, :] = sk[p, :, :] - jnp.concatenate([share[:, :QN], share[:, QN:]], 0)
        q_back = (q_blocks * (inverse * 0.125)).astype(BF16)
        g_back = (g_blocks * inverse).astype(BF16)
        dq = jnp.zeros((LANES, 2 * QN), F32)
        for c in range(N_CHUNK):
            here = slice(c * KEYS, (c + 1) * KEYS)
            rows = slice(c * CHUNK, (c + 1) * CHUNK)
            k_here = ext[0, rows, span, :].reshape(KEYS, LANES)
            v_here = ext[1, rows, span, :].reshape(KEYS, LANES)
            prob = dot(v_here, g_low) - delta
            score = (u_s[here, :].astype(F32) * prob).astype(BF16)
            dk = dot(score, q_back, NT)
            dv = dot(e_s[here, :], g_back, NT)
            dq = dq + dot(k_here, score, TN)
            acc[p, 0, rows, span, :] += dk.reshape(CHUNK, SPAN, LANES)
            acc[p, 1, rows, span, :] += dv.reshape(CHUNK, SPAN, LANES)
        dq = dq * (inverse * 0.125)
        out_s[1, p, :, cols, :] = own_heads(dq).T.reshape(ROWS, TILE, LANES).astype(BF16)

    def gs_copy(p, side):
        return pltpu.make_async_remote_copy(
            src_ref=gstrip_to.at[p, side],
            dst_ref=gstrip_from.at[p, 1 - side],
            send_sem=gs_send.at[p, side],
            recv_sem=gs_recv.at[p, 1 - side],
            device_id=sides[side],
            device_id_type=MESH,
        )

    def send_strips(p, side):
        first = (0, COLS + WIDE)[side]
        for rp in range(EXT_ROWS // 2):
            for i in range(2):
                both = acc[p, i, 2 * rp : 2 * rp + 2, first : first + WIDE, :]
                gstrip_to[p, side, rp, i] = both.reshape(2 * WIDE, LANES).astype(BF16)
        gs_copy(p, side).start()

    def rim_copy(p, side):
        return pltpu.make_async_remote_copy(
            src_ref=rim_to.at[p, side],
            dst_ref=rim_from.at[p, 1 - side],
            send_sem=rim_send.at[p, side],
            recv_sem=rim_recv.at[p, 1 - side],
            device_id=(up, down)[side],
            device_id_type=MESH,
        )

    def stage_c(p):
        for side in range(2):
            gs_copy(p, side).wait_recv()
        for rp in range(EXT_ROWS // 2):
            for i in range(2):
                for side in range(2):
                    first = (WIDE, COLS)[side]
                    came = gstrip_from[p, side, rp, i].astype(F32).reshape(2, WIDE, LANES)
                    acc[p, i, 2 * rp : 2 * rp + 2, first : first + WIDE, :] += came
        for i in range(2):
            for r in range(RADIUS):
                rim_to[p, 0, i, r] = acc[p, i, r, WIDE : WIDE + COLS, :].astype(BF16)
                rim_to[p, 1, i, r] = acc[p, i, RADIUS + ROWS + r, WIDE : WIDE + COLS, :].astype(BF16)
        for side in range(2):
            rim_copy(p, side).start()

    def store(i, p):
        return pltpu.make_async_copy(
            out_s.at[i, p],
            (o_hbm, dq_hbm, dk_hbm, dv_hbm)[i].at[
                :, :, pl.ds(pl.multiple_of(p * LANES, LANES), LANES)
            ],
            out_sem.at[i, p],
        )

    def stage_d(p):
        for side in range(2):
            rim_copy(p, side).wait_recv()
        for i in range(2):
            for r in range(ROWS):
                total = acc[p, i, RADIUS + r, WIDE : WIDE + COLS, :]
                if r < RADIUS:
                    total = total + rim_from[p, 0, i, r].astype(F32)
                if r >= ROWS - RADIUS:
                    total = total + rim_from[p, 1, i, r - (ROWS - RADIUS)].astype(F32)
                out_s[2 + i, p, r] = total.astype(BF16)
        for i in (2, 3):
            store(i, p).start()

    sk[...] = jnp.zeros_like(sk)
    stage_a(0)

    def step(p, carry):
        for i in (0, 3):
            load(i, p).wait()
        stage_ext(p)
        attend(p, 0)
        send_strips(p, 0)

        @pl.when(p < PAIRS - 1)
        def _():
            stage_a(p + 1)

        @pl.when(p > 0)
        def _():
            stage_c(p - 1)

        attend(p, 1)
        send_strips(p, 1)
        for i in (0, 1):
            store(i, p).start()

        @pl.when(p > 1)
        def _():
            stage_d(p - 2)

        return carry

    lax.fori_loop(0, PAIRS, step, 0)

    groups = ((N_LAT, lat_peer), (4, quad_peer), (N_Z, z_peer))

    def sk_copy(stage, d):
        size, peer = groups[stage]
        return pltpu.make_async_remote_copy(
            src_ref=sk_all.at[stage, 0],
            dst_ref=sk_all.at[stage, d],
            send_sem=sk_send.at[stage, d],
            recv_sem=sk_recv.at[stage, d],
            device_id=peer(d),
            device_id_type=MESH,
        )

    def sk_put(stage):
        for d in range(1, groups[stage][0]):
            sk_copy(stage, d).start()

    def sk_get(stage):
        for d in range(1, groups[stage][0]):
            sk_copy(stage, d).wait_recv()
        return jnp.sum(sk_all[stage, : groups[stage][0]], axis=0)

    sk_all[0, 0] = sk[...].reshape(2 * PAIRS, QN)
    sk_put(0)
    stage_c(PAIRS - 1)
    stage_d(PAIRS - 2)
    sk_all[1, 0] = sk_get(0)
    sk_put(1)
    sk_all[2, 0] = sk_get(1)

    @pl.when(z < N_Z - 1)
    def _():
        pl.semaphore_wait(met, N_Z - 1 - z)

    sk_put(2)
    stage_d(PAIRS - 1)
    sg_ref[...] = jnp.broadcast_to(jnp.sum(sk_get(2), axis=1, keepdims=True), (2 * PAIRS, QN))

    for p in range(PAIRS):
        for i in range(4):
            store(i, p).wait()
        for side in range(2):
            for i in range(2):
                lat_copy(p, i, side).wait_send()
            for part in range(3):
                strip_copy(p, side, part).wait_send()
            gs_copy(p, side).wait_send()
            rim_copy(p, side).wait_send()
    for stage in range(3):
        for d in range(1, groups[stage][0]):
            sk_copy(stage, d).wait_send()


def on_device(queries, keys, values, grad_out, sink_logits):
    shape = jax.ShapeDtypeStruct(queries.shape, BF16)
    anywhere = pl.BlockSpec(memory_space=pl.ANY)
    dma = pltpu.SemaphoreType.DMA
    attended, query_grad, key_grad, value_grad, sink_grad = pl.pallas_call(
        kernel,
        out_shape=(shape,) * 4 + (jax.ShapeDtypeStruct((2 * PAIRS, QN), F32),),
        in_specs=[anywhere] * 4 + [pl.BlockSpec(memory_space=pltpu.SMEM)],
        out_specs=(anywhere,) * 4 + (pl.BlockSpec(memory_space=pltpu.VMEM),),
        scratch_shapes=[
            pltpu.VMEM((PAIRS, ROWS, COLS, LANES), BF16),
            pltpu.VMEM((2, PAIRS, ROWS, COLS, LANES), BF16),
            pltpu.VMEM((PAIRS, ROWS, COLS, LANES), BF16),
            pltpu.VMEM((2, EXT_ROWS, EXT_COLS, LANES), BF16),
            pltpu.VMEM((PAIRS, 2, RADIUS, COLS, LANES), BF16),
            pltpu.VMEM((PAIRS, 2, RADIUS, COLS, LANES), BF16),
            pltpu.VMEM((EXT_ROWS * SPAN, QN), F32),
            pltpu.VMEM((PAIRS, 2, EXT_ROWS // 2, 2, 2 * WIDE, LANES), BF16),
            pltpu.VMEM((PAIRS, 2, EXT_ROWS // 2, 2, 2 * WIDE, LANES), BF16),
            pltpu.VMEM((PAIRS, 2, EXT_ROWS // 2, 2, 2 * WIDE, LANES), BF16),
            pltpu.VMEM((PAIRS, 2, EXT_ROWS // 2, 2, 2 * WIDE, LANES), BF16),
            pltpu.VMEM((PAIRS, 2, 2, RADIUS, COLS, LANES), BF16),
            pltpu.VMEM((PAIRS, 2, 2, RADIUS, COLS, LANES), BF16),
            pltpu.VMEM((PAIRS, 2, EXT_ROWS, EXT_COLS, LANES), F32),
            pltpu.VMEM((EXT_ROWS * SPAN, 2 * QN), BF16),
            pltpu.VMEM((EXT_ROWS * SPAN, 2 * QN), BF16),
            pltpu.VMEM((4, PAIRS, ROWS, COLS, LANES), BF16),
            pltpu.VMEM((PAIRS, 2, QN), F32),
            pltpu.VMEM((3, N_LAT, 2 * PAIRS, QN), F32),
            dma((4, PAIRS)),
            dma((4, PAIRS)),
            dma((PAIRS, 2, 2)),
            dma((PAIRS, 2, 2)),
            dma((PAIRS, 2, 3)),
            dma((PAIRS, 2, 3)),
            dma((PAIRS, 2)),
            dma((PAIRS, 2)),
            dma((PAIRS, 2)),
            dma((PAIRS, 2)),
            dma((3, N_LAT)),
            dma((3, N_LAT)),
            pltpu.SemaphoreType.REGULAR((2,)),
            pltpu.SemaphoreType.REGULAR,
        ],
        compiler_params=pltpu.CompilerParams(
            collective_id=0, has_side_effects=True, vmem_limit_bytes=60 * 1024 * 1024
        ),
    )(queries, keys, values, grad_out, sink_logits)
    return attended, query_grad, key_grad, value_grad, sink_grad[:, 0]


def solution(mesh):
    cells = P("lat", "lon", None)
    return jax.shard_map(
        on_device,
        mesh=mesh,
        in_specs=(cells,) * 4 + (P(),),
        out_specs=(cells,) * 4 + (P(),),
        check_vma=False,
    )
```

time: 306 us -> 62.5 us (0.20)
  blocking collectives: 79.9 us -> 0 us
  matrix products: 73.4 us -> 0 us
  local copies, waits for them, and re-layouts: 75.2 us -> 5.8 us
  Pallas kernels: 0 us -> 55.8 us
  other arithmetic: 33.4 us -> 0 us
  starting transfers between devices: 26.8 us -> 0 us
  waiting for transfers between devices: 8.27 us -> 0 us
  between operations: 7.11 us -> 0.65 us
    psum x1 -> x0, blocking collectives: 79.9 us -> none  [on_device(): sink_grad = lax.psum(sink_local, ('lat', 'lon'))]
    dot_general x48 -> x0, matrix products: 73.4 us -> none  [the longest x8 19.7 us: one_band(): jnp.dot(grad_head, value_head.T, preferred_element_type=jnp.float32)]
    pallas_call x0 -> x1, Pallas kernels: none -> 55.8 us  [on_device(): pl.pallas_call(kernel, out_shape=(shape,) * 4 + (jax.ShapeDtypeStruct((2...]
    ppermute x8 -> x0, starting transfers between devices: 26.8 us -> none  [the longest x2 9.05 us: shifted(): lax.ppermute(value, axis, [(i, (i + by) % size) for i in range(size)])]
    convert_element_type x17 -> x0, local copies, waits for them, and re-layouts: 18.3 us -> none  [the longest x8 9.93 us: one_band(): score_grad = (attention * (prob_grad - delta_sum[:, None]) * (1.0 - squas...]
    unnamed x205 -> x12, local copies, waits for them, and re-layouts: 21.7 us -> 5.18 us
    slice x6 -> x1, local copies, waits for them, and re-layouts: 12.9 us -> 0.62 us  [on_device(): return (attended, query_grad, key_grad, value_grad, sink_grad[:, 0])]
    concatenate x5 -> x0, local copies, waits for them, and re-layouts: 11.3 us -> none  [the longest x1 2.76 us: one_band(): jnp.concatenate(value_pieces, axis=1)]
  transfers between devices with their start and end apart: 8 -> 0, of which waited for: 4 -> 0; matrix products, arithmetic and copies ran while one was open for 7% -> 0% of each run, Pallas kernels for 0% -> 0%
where the time goes in v1:
time: 62.5 us; the launch traced here: 62.3 us
  Pallas kernels  55.8 us (89%)
  local copies, waits for them, and re-layouts  5.8 us (9%)
  between operations  0.65 us (1%)
    pallas_call x1, Pallas kernels, on_device(): pl.pallas_call(kernel, out_shape=(shape,) * 4 + (jax.ShapeDtypeStruct((2...  55.8 us
    unnamed x12, local copies, waits for them, and re-layouts  5.18 us

profile of v1, /device:TPU:1, one launch (start us, length us, event | category | flops | bytes accessed | tf_op | source)
XLA Modules:
  0.0 62.3 jit_solution(10799774868702959382)
XLA Ops:
  0.6 55.8 %shard_map.92 = (bf16[8,32,512]{2,1,0:T(8,128)(2,1)}, bf16[8,32,512]{2,1,0:T(8,128)(2,1)}, bf16[8,32,512]{2,1,0:T(8,128)(2,1)}, bf16[8,32,512]{2,1,0:T(8,128)(2,1)}, f32[8,128]{1,0:T(8,128)}) custom-call(bf16[8,32,512]{2,1,0:T(8,128)(2,1)} %q_hbm.1, bf16[8,32,512]{2,1,0:T(8,128)(2,1)} %k_hbm.1, bf16[8,32,512]{2,1,0:T(8,128)(2,1)} %v_hbm.1, ...), custom_call_target="tpu_custom_call" | custom-call | tf_op jit(solution)/shard_map/pallas_call | solution.py:446
  56.4 0.0 copy-start.3
  56.5 0.7 %copy-done.3 = f32[8,128]{1,0:T(8,128)S(1)} copy-done((f32[8,128]{1,0:T(8,128)S(1)}, f32[8,128]{1,0:T(8,128)}, u32[]{:S(2)}) %copy-start.3) | copy-done | bytes 4120
  57.1 0.6 %slice_reduce_fusion = f32[8]{0:T(128)} fusion(f32[8,128]{1,0:T(8,128)S(1)} %copy-done.3), kind=kLoop, calls=%fused_computation | loop fusion | bytes 64 | tf_op jit(solution)/shard_map/slice | solution.py:490
  57.7 0.0 copy-start.2
  57.8 1.7 %copy.14 = bf16[8,32,512]{2,1,0:T(8,128)(2,1)} copy(bf16[8,32,512]{2,1,0:T(8,128)(2,1)} %get-tuple-element.20) | data formatting | bytes 524288
  59.5 0.0 copy-done.2
  59.5 0.0 copy-start.1
  59.5 0.7 %copy.15 = bf16[8,32,512]{2,1,0:T(8,128)(2,1)} copy(bf16[8,32,512]{2,1,0:T(8,128)(2,1)S(1)} %copy-done.2) | data formatting | bytes 524288
  60.2 0.3 copy-done.1
  60.5 0.0 copy-start
  60.5 0.7 %copy.16 = bf16[8,32,512]{2,1,0:T(8,128)(2,1)} copy(bf16[8,32,512]{2,1,0:T(8,128)(2,1)S(1)} %copy-done.1) | data formatting | bytes 524288
  61.2 0.3 copy-done
  61.6 0.7 %copy.17 = bf16[8,32,512]{2,1,0:T(8,128)(2,1)} copy(bf16[8,32,512]{2,1,0:T(8,128)(2,1)S(1)} %copy-done) | data formatting | bytes 524288
Async XLA Ops:
  56.4 0.7 %copy-start.3 = (f32[8,128]{1,0:T(8,128)S(1)}, f32[8,128]{1,0:T(8,128)}, u32[]{:S(2)}) copy-start(f32[8,128]{1,0:T(8,128)} %get-tuple-element.14) | copy-start | bytes 12292
  57.7 1.7 %copy-start.2 = (bf16[8,32,512]{2,1,0:T(8,128)(2,1)S(1)}, bf16[8,32,512]{2,1,0:T(8,128)(2,1)}, u32[]{:S(2)}) copy-start(bf16[8,32,512]{2,1,0:T(8,128)(2,1)} %get-tuple-element.21) | copy-start | bytes 786436
  59.5 1.0 %copy-start.1 = (bf16[8,32,512]{2,1,0:T(8,128)(2,1)S(1)}, bf16[8,32,512]{2,1,0:T(8,128)(2,1)}, u32[]{:S(2)}) copy-start(bf16[8,32,512]{2,1,0:T(8,128)(2,1)} %get-tuple-element.22) | copy-start | bytes 786436
  60.5 1.0 %copy-start = (bf16[8,32,512]{2,1,0:T(8,128)(2,1)S(1)}, bf16[8,32,512]{2,1,0:T(8,128)(2,1)}, u32[]{:S(2)}) copy-start(bf16[8,32,512]{2,1,0:T(8,128)(2,1)} %get-tuple-element.23) | copy-start | bytes 786436

commit v2 on v1

v2 whole, which is shorter than its diff:
```python
import functools
import math

import jax
import jax.numpy as jnp
from jax import lax
from jax.experimental import pallas as pl
from jax.experimental.pallas import tpu as pltpu
from jax.sharding import PartitionSpec as P

WIN = 13
RADIUS = WIN // 2
SOFTCAP = 8.0
PAIRS = 4
ROWS = 8
COLS = 32
WIDE = 8
EXT_ROWS = ROWS + 2 * RADIUS
EXT_COLS = COLS + 2 * WIDE
TILE = 16
SPAN = TILE + 2 * WIDE
KEYS = EXT_ROWS * SPAN
QN = ROWS * TILE
LANES = 128
N_LAT = 8
N_LON = 32
N_Z = 8
N_NEAR = 2 * N_LAT
N_FAR = 2 * N_Z
MESH = pl.DeviceIdType.MESH
BF16 = jnp.bfloat16
F32 = jnp.float32
EXP2_RATE = SOFTCAP * math.log2(math.e)

NT = (((1,), (1,)), ((), ()))
TN = (((0,), (0,)), ((), ()))


def dot(a, b, dims=(((1,), (0,)), ((), ()))):
    return lax.dot_general(a, b, dims, preferred_element_type=F32)


def head_blocks(turned):
    first = lax.broadcasted_iota(jnp.int32, (LANES, QN), 0) < LANES // 2
    return jnp.concatenate(
        [jnp.where(first, turned, 0.0), jnp.where(first, 0.0, turned)], axis=1
    )


def own_heads(both):
    first = lax.broadcasted_iota(jnp.int32, (LANES, QN), 0) < LANES // 2
    return jnp.where(first, both[:, :QN], both[:, QN:])


def kernel(
    q_hbm, k_hbm, v_hbm, g_hbm, sink_hbm,
    o_ref, dq_ref, dk_ref, dv_ref, sg_ref,
    sink_ref, q_s, kv_s, g_s, ext, top, bot, mask,
    strip_to, strip_from, gstrip_to, gstrip_from, rim_to, rim_from,
    acc, e_s, u_s, prob_s, rate, sk, sk_plane, sk_z,
    sink_sem, in_sem, lat_send, lat_recv, strip_send, strip_recv,
    gs_send, gs_recv, rim_send, rim_recv, skp_send, skp_recv, skz_send, skz_recv, entered, met,
):
    a = lax.axis_index("lat")
    b = lax.axis_index("lon")
    up = (lax.rem(a + N_LAT - 1, N_LAT), b)
    down = (lax.rem(a + 1, N_LAT), b)
    left = (a, lax.rem(b + N_LON - 1, N_LON))
    right = (a, lax.rem(b + 1, N_LON))
    sides = (left, right)
    column = lax.rem(b, 2 * N_Z)
    z = column // 2
    is_first = column == 0
    is_last = column == 2 * N_Z - 1

    core = lax.rem(b, 2)
    crossing = (left[1], right[1])

    def diagonal(side, da):
        return (lax.rem(a + da + N_LAT, N_LAT), crossing[side])

    half = b // (2 * N_Z)

    def near_peer(d):
        other = lax.rem(2 * a + core + d, N_NEAR)
        return (other // 2, lax.rem(other, 2) + 2 * z + 2 * N_Z * half)

    def across(dz, dh):
        return (a, core + 2 * lax.rem(z + dz + N_Z, N_Z) + 2 * N_Z * lax.rem(half + dh, 2))

    def far_peer(d):
        other = lax.rem(2 * z + half + d, N_FAR)
        return (a, core + 2 * (other // 2) + 2 * N_Z * lax.rem(other, 2))

    def load(i, p):
        src = (q_hbm, k_hbm, v_hbm, g_hbm)[i]
        dst = (q_s, kv_s.at[0], kv_s.at[1], g_s)[i]
        return pltpu.make_async_copy(
            src.at[:, :, pl.ds(pl.multiple_of(p * LANES, LANES), LANES)], dst.at[p], in_sem.at[i, p]
        )

    for p in range(PAIRS):
        for i in (1, 2):
            load(i, p).start()
    for p in range(PAIRS):
        for i in (0, 3):
            load(i, p).start()

    sink_copy = pltpu.make_async_copy(sink_hbm, sink_ref, sink_sem)
    sink_copy.start()
    barrier = pltpu.get_barrier_semaphore()

    def greet(device):
        pl.semaphore_signal(barrier, inc=1, device_id=device, device_id_type=MESH)

    for d in range(1, N_NEAR):
        greet(near_peer(d))
    greet(across(0, 1))

    @pl.when((core == 1) & jnp.logical_not(is_last))
    def _():
        greet(right)

    @pl.when(is_first)
    def _():
        for da in (-1, 0, 1):
            greet(diagonal(0, da))

    for d in range(1, N_Z):
        @pl.when(z + d < N_Z)
        def _():
            greet(across(d, 0))
            greet(across(d, 1))

    answers = ((core == 0) & jnp.logical_not(is_first)) | is_last
    pl.semaphore_wait(barrier, N_NEAR + 2 * z + jnp.where(is_last, 3, jnp.where(answers, 1, 0)))

    def lat_copy(p, i, side):
        src = (k_hbm, v_hbm)[i]
        first_row = (0, ROWS - RADIUS)[side]
        return pltpu.make_async_remote_copy(
            src_ref=src.at[
                first_row : first_row + RADIUS, :, pl.ds(pl.multiple_of(p * LANES, LANES), LANES)
            ],
            dst_ref=(bot, top)[side].at[p, i],
            send_sem=lat_send.at[p, i, side],
            recv_sem=lat_recv.at[p, i, side],
            device_id=(up, down)[side],
            device_id_type=MESH,
        )

    def send_rows(p):
        for i in range(2):
            for side in range(2):
                lat_copy(p, i, side).start()

    send_rows(0)
    send_rows(1)

    @pl.when((core == 0) & jnp.logical_not(is_first))
    def _():
        pl.semaphore_signal(entered, inc=1, device_id=left, device_id_type=MESH)

    @pl.when(is_last)
    def _():
        for da in (-1, 0, 1):
            pl.semaphore_signal(entered, inc=1, device_id=diagonal(1, da), device_id_type=MESH)

    for d in range(1, N_Z):
        @pl.when(z - d >= 0)
        def _():
            for dh in range(2):
                pl.semaphore_signal(met, inc=1, device_id=across(-d, dh), device_id_type=MESH)

    key = lax.broadcasted_iota(jnp.int32, (EXT_ROWS * SPAN, QN), 0)
    query = lax.broadcasted_iota(jnp.int32, (EXT_ROWS * SPAN, QN), 1)
    key_row = key // SPAN - RADIUS
    row_gap = key_row - query // TILE
    col_gap = lax.rem(key, SPAN) - WIDE - lax.rem(query, TILE)
    whole_row = a * ROWS + key_row
    meets = (
        (row_gap >= -RADIUS) & (row_gap <= RADIUS) & (col_gap >= -RADIUS) & (col_gap <= RADIUS)
        & (whole_row >= 0) & (whole_row < N_LAT * ROWS)
    )
    mask[...] = jnp.where(meets, 1.0, 0.0)

    def rows_of(p, i, r):
        if r < RADIUS:
            return top[p, i, r].astype(F32)
        if r < RADIUS + ROWS:
            return kv_s[i, p, r - RADIUS].astype(F32)
        return bot[p, i, r - RADIUS - ROWS].astype(F32)

    def pack(p, first, last):
        for rp in range(first, last):
            for i in range(2):
                upper, lower = rows_of(p, i, 2 * rp), rows_of(p, i, 2 * rp + 1)
                strip_to[p, 0, rp, i] = jnp.concatenate([upper[:WIDE], lower[:WIDE]], 0).astype(BF16)
                strip_to[p, 1, rp, i] = jnp.concatenate(
                    [upper[COLS - WIDE :], lower[COLS - WIDE :]], 0
                ).astype(BF16)

    spans = ((3, 4), (0, 3), (7, 3))
    direct = (is_first, is_last)

    def strip_copy(p, side, part):
        first, count = spans[part]
        source, to = first, a
        if part == 1:
            source, to = jnp.where(direct[side], 4, 0), jnp.where(direct[side], lax.rem(a + 1, N_LAT), a)
        if part == 2:
            source = jnp.where(direct[side], 3, 7)
            to = jnp.where(direct[side], lax.rem(a + N_LAT - 1, N_LAT), a)
        return pltpu.make_async_remote_copy(
            src_ref=strip_to.at[p, side, pl.ds(source, count)],
            dst_ref=strip_from.at[p, 1 - side, first : first + count],
            send_sem=strip_send.at[p, side, part],
            recv_sem=strip_recv.at[p, 1 - side, part],
            device_id=(to, sides[side][1]),
            device_id_type=MESH,
        )

    for p in range(PAIRS):
        for i in (1, 2):
            load(i, p).wait()
        pack(p, 3, 7)

    @pl.when(is_last)
    def _():
        for p in range(PAIRS):
            for part in (1, 2):
                strip_copy(p, 1, part).start()

    send_rows(2)
    send_rows(3)
    sure = ((core == 1) | (core == 0) & jnp.logical_not(is_first), (core == 0) | is_last)
    for side in range(2):
        @pl.when(sure[side])
        def _():
            for p in range(PAIRS):
                strip_copy(p, side, 0).start()

    acc[...] = jnp.zeros_like(acc)
    sk[...] = jnp.zeros_like(sk)

    def stage_a(p):
        for i in range(2):
            for side in range(2):
                lat_copy(p, i, side).wait_recv()
        pack(p, 0, 3)
        pack(p, 7, 10)
        for side in range(2):
            @pl.when(jnp.logical_not(direct[side]))
            def _():
                for part in (1, 2):
                    strip_copy(p, side, part).start()

    def ext_middle(p):
        for r in range(EXT_ROWS):
            for i in range(2):
                ext[i, r, TILE : 2 * TILE] = rows_of(p, i, r)[WIDE : WIDE + TILE].astype(BF16)

    def ext_sides(p):
        for side in range(2):
            for part in range(3):
                strip_copy(p, side, part).wait_recv()
        for rp in range(EXT_ROWS // 2):
            for i in range(2):
                west = strip_from[p, 0, rp, i].astype(F32)
                east = strip_from[p, 1, rp, i].astype(F32)
                for j in range(2):
                    r = 2 * rp + j
                    half = slice(j * WIDE, (j + 1) * WIDE)
                    center = rows_of(p, i, r)
                    ext[i, r, :TILE] = jnp.concatenate([west[half], center[:WIDE]], 0).astype(BF16)
                    ext[i, r, 2 * TILE :] = jnp.concatenate(
                        [center[COLS - WIDE :], east[half]], 0
                    ).astype(BF16)

    def place(tile):
        at = tile * TILE
        return slice(at, at + TILE), slice(at, at + SPAN)

    def lanes(p):
        return pl.ds(pl.multiple_of(p * LANES, LANES), LANES)

    def turned(ref, p, cols):
        return head_blocks(ref[p, :, cols, :].reshape(QN, LANES).astype(F32).T)

    def forward(p, tile):
        cols, span = place(tile)
        q_low = (turned(q_s, p, cols) * (1.0 / 64.0)).astype(BF16)
        lane = lax.broadcasted_iota(jnp.int32, (1, 2 * QN), 1)
        sink = jnp.exp(jnp.where(lane < QN, sink_ref[2 * p], sink_ref[2 * p + 1]))
        k_here = ext[0, :, span, :].reshape(KEYS, LANES)
        v_here = ext[1, :, span, :].reshape(KEYS, LANES)
        g_blocks = turned(g_s, p, cols)
        squashed = jnp.tanh(dot(k_here, q_low))
        meets_here = mask[...]
        weight = jnp.exp2(squashed * EXP2_RATE) * jnp.concatenate([meets_here, meets_here], 1)
        total = jnp.sum(weight.reshape(KEYS // 8, 8, 2 * QN), axis=0)
        weight_low = weight.astype(BF16)
        e_s[tile] = weight_low
        u_s[tile] = (weight * (1.0 - squashed * squashed)).astype(BF16)
        prob_s[tile] = dot(v_here, g_blocks.astype(BF16))
        out = dot(v_here, weight_low, TN)
        inverse = 1.0 / (jnp.sum(total, axis=0, keepdims=True) + sink)
        out = out * inverse
        delta = jnp.sum(g_blocks * out, axis=0, keepdims=True)
        rate[tile, 0] = jnp.broadcast_to(inverse, (8, 2 * QN))
        rate[tile, 1] = jnp.broadcast_to(delta, (8, 2 * QN))
        o_ref[:, cols, lanes(p)] = own_heads(out).T.reshape(ROWS, TILE, LANES).astype(BF16)
        share = sink * inverse * delta
        sk[p, :, :] = sk[p, :, :] - jnp.concatenate([share[:, :QN], share[:, QN:]], 0)

    def backward(p, tile):
        cols, span = place(tile)
        inverse = rate[tile, 0, 0:1, :]
        delta = rate[tile, 1, 0:1, :]
        g_blocks = turned(g_s, p, cols)
        q_back = (turned(q_s, p, cols) * (inverse * 0.125)).astype(BF16)
        g_back = (g_blocks * inverse).astype(BF16)
        k_here = ext[0, :, span, :].reshape(KEYS, LANES)
        score = (u_s[tile].astype(F32) * (prob_s[tile] - delta)).astype(BF16)
        dk = dot(score, q_back, NT)
        dv = dot(e_s[tile], g_back, NT)
        dq = dot(k_here, score, TN)
        acc[p, 0, :, span, :] += dk.reshape(EXT_ROWS, SPAN, LANES)
        acc[p, 1, :, span, :] += dv.reshape(EXT_ROWS, SPAN, LANES)
        dq = dq * (inverse * 0.125)
        dq_ref[:, cols, lanes(p)] = own_heads(dq).T.reshape(ROWS, TILE, LANES).astype(BF16)

    def gs_copy(p, side, part):
        first, count = spans[part]
        to, lands = a, first
        if part == 1:
            to = jnp.where(direct[side], lax.rem(a + N_LAT - 1, N_LAT), a)
            lands = jnp.where(direct[side], 7, 0)
        if part == 2:
            to = jnp.where(direct[side], lax.rem(a + 1, N_LAT), a)
            lands = jnp.where(direct[side], 0, 7)
        sem = part if part == 0 else jnp.where(direct[side], 3 - part, part)
        return pltpu.make_async_remote_copy(
            src_ref=gstrip_to.at[p, side, first : first + count],
            dst_ref=gstrip_from.at[p, 1 - side, pl.ds(lands, count)],
            send_sem=gs_send.at[p, side, sem],
            recv_sem=gs_recv.at[p, 1 - side, sem],
            device_id=(to, sides[side][1]),
            device_id_type=MESH,
        )

    def send_strips(p, side):
        first = side * (COLS + WIDE)
        for rp in range(EXT_ROWS // 2):
            for i in range(2):
                both = acc[p, i, 2 * rp : 2 * rp + 2, first : first + WIDE, :]
                gstrip_to[p, side, rp, i] = both.reshape(2 * WIDE, LANES).astype(BF16)

    def start_strips(p):
        for side in range(2):
            for part in (1, 2, 0):
                gs_copy(p, side, part).start()

    def rim_copy(p, side):
        return pltpu.make_async_remote_copy(
            src_ref=rim_to.at[p, side],
            dst_ref=rim_from.at[p, 1 - side],
            send_sem=rim_send.at[p, side],
            recv_sem=rim_recv.at[p, 1 - side],
            device_id=(up, down)[side],
            device_id_type=MESH,
        )

    def add_strip(p, side, rp, row):
        first = (WIDE, COLS)[side]
        for i in range(2):
            came = gstrip_from[p, side, rp, i].astype(F32).reshape(2, WIDE, LANES)
            acc[p, i, pl.ds(row, 2), first : first + WIDE, :] += came

    def stage_c(p):
        for side in range(2):
            @pl.when(jnp.logical_not(direct[side]))
            def _():
                for part in (1, 2):
                    gs_copy(p, 1 - side, part).wait_recv()
                for rp in (0, 1, 2, 7, 8, 9):
                    add_strip(p, side, rp, 2 * rp)
        for i in range(2):
            for r in range(RADIUS):
                rim_to[p, 0, i, r] = acc[p, i, r, WIDE : WIDE + COLS, :].astype(BF16)
                rim_to[p, 1, i, r] = acc[p, i, RADIUS + ROWS + r, WIDE : WIDE + COLS, :].astype(BF16)
        for side in range(2):
            rim_copy(p, side).start()

    def stage_d(p):
        for side in range(2):
            gs_copy(p, 1 - side, 0).wait_recv()
            for rp in (3, 4, 5, 6):
                add_strip(p, side, rp, 2 * rp)

            @pl.when(direct[side])
            def _():
                for part in (1, 2):
                    gs_copy(p, 1 - side, part).wait_recv()
                for rp in range(3):
                    add_strip(p, side, rp, 2 * rp + RADIUS)
                    add_strip(p, side, rp + 7, 2 * rp + RADIUS + 2)
        for side in range(2):
            rim_copy(p, side).wait_recv()
        for i in range(2):
            for r in range(ROWS):
                total = acc[p, i, RADIUS + r, WIDE : WIDE + COLS, :]
                if r < RADIUS:
                    total = total + rim_from[p, 0, i, r].astype(F32)
                if r >= ROWS - RADIUS:
                    total = total + rim_from[p, 1, i, r - (ROWS - RADIUS)].astype(F32)
                (dk_ref, dv_ref)[i][r, :, lanes(p)] = total.astype(BF16)

    def skp_copy(d):
        return pltpu.make_async_remote_copy(
            src_ref=sk_plane.at[0], dst_ref=sk_plane.at[d],
            send_sem=skp_send.at[d], recv_sem=skp_recv.at[d],
            device_id=near_peer(d), device_id_type=MESH,
        )

    def skz_copy(d):
        return pltpu.make_async_remote_copy(
            src_ref=sk_z.at[0], dst_ref=sk_z.at[d],
            send_sem=skz_send.at[d], recv_sem=skz_recv.at[d],
            device_id=far_peer(d), device_id_type=MESH,
        )

    sink_copy.wait()

    @pl.when((core == 1) & jnp.logical_not(is_last))
    def _():
        pl.semaphore_wait(entered, 1)
        for p in range(PAIRS):
            strip_copy(p, 1, 0).start()

    stage_a(0)
    stage_a(1)

    @pl.when(is_first)
    def _():
        pl.semaphore_wait(entered, 3)
        for p in range(PAIRS):
            for part in (1, 2, 0):
                strip_copy(p, 0, part).start()
        stage_a(2)
        stage_a(3)

    def gather(p):
        for i in (0, 3):
            load(i, p).wait()
        ext_middle(p)
        ext_sides(p)

    def forward_both(p):
        forward(p, 0)
        forward(p, 1)

    def backward_both(p):
        backward(p, 0)
        backward(p, 1)
        send_strips(p, 0)
        send_strips(p, 1)
        start_strips(p)

    def step(p, carry):
        gather(p)
        forward_both(p)
        backward_both(p)

        @pl.when((p < PAIRS - 2) & jnp.logical_not(is_first))
        def _():
            stage_a(p + 2)

        @pl.when(p > 0)
        def _():
            stage_c(p - 1)

        return carry

    lax.fori_loop(0, PAIRS - 1, step, 0)
    gather(PAIRS - 1)
    forward_both(PAIRS - 1)
    sk_plane[0] = sk[...].reshape(2 * PAIRS, QN)
    for d in range(1, N_NEAR):
        skp_copy(d).start()
    backward_both(PAIRS - 1)
    stage_c(PAIRS - 2)
    stage_c(PAIRS - 1)
    for d in range(1, N_NEAR):
        skp_copy(d).wait_recv()
    sk_z[0] = jnp.sum(sk_plane[...], axis=0)

    @pl.when(z < N_Z - 1)
    def _():
        pl.semaphore_wait(met, 2 * (N_Z - 1 - z))

    for d in range(1, N_FAR):
        skz_copy(d).start()

    def finish(p, carry):
        stage_d(p)
        return carry

    lax.fori_loop(0, PAIRS, finish, 0)
    for d in range(1, N_FAR):
        skz_copy(d).wait_recv()
    sg_ref[...] = jnp.broadcast_to(
        jnp.sum(jnp.sum(sk_z[...], axis=0), axis=1, keepdims=True), (2 * PAIRS, QN)
    )

    for p in range(PAIRS):
        for side in range(2):
            for i in range(2):
                lat_copy(p, i, side).wait_send()
            for part in range(3):
                strip_copy(p, side, part).wait_send()
                gs_copy(p, side, part).wait_send()
            rim_copy(p, side).wait_send()
    for d in range(1, N_NEAR):
        skp_copy(d).wait_send()
    for d in range(1, N_FAR):
        skz_copy(d).wait_send()


def place_results(o_ref, dq_ref, dk_ref, dv_ref, sg_ref, o_out, dq_out, dk_out, dv_out, sg_out, sem):
    sources = (o_ref, dq_ref, dk_ref, dv_ref)
    stores = [
        pltpu.make_async_copy(sources[i], there, sem.at[i])
        for i, there in enumerate((o_out, dq_out, dk_out, dv_out))
    ]
    for store in stores:
        store.start()
    row = lax.broadcasted_iota(jnp.int32, (2 * PAIRS, QN), 0)
    lane = lax.broadcasted_iota(jnp.int32, (2 * PAIRS, QN), 1)
    sg_out[...] = jnp.sum(jnp.where(row == lane, sg_ref[...], 0.0), axis=0)[: 2 * PAIRS]
    for store in stores:
        store.wait()


def on_device(queries, keys, values, grad_out, sink_logits):
    shape = jax.ShapeDtypeStruct(queries.shape, BF16)
    anywhere = pl.BlockSpec(memory_space=pl.ANY)
    dma = pltpu.SemaphoreType.DMA
    vmem = pl.BlockSpec(memory_space=pltpu.VMEM)
    results = pl.pallas_call(
        kernel,
        out_shape=(pltpu.VMEM(queries.shape, BF16),) * 4 + (pltpu.VMEM((2 * PAIRS, QN), F32),),
        in_specs=[anywhere] * 5,
        out_specs=(vmem,) * 5,
        scratch_shapes=[
            pltpu.SMEM((2 * PAIRS,), F32),
            pltpu.VMEM((PAIRS, ROWS, COLS, LANES), BF16),
            pltpu.VMEM((2, PAIRS, ROWS, COLS, LANES), BF16),
            pltpu.VMEM((PAIRS, ROWS, COLS, LANES), BF16),
            pltpu.VMEM((2, EXT_ROWS, EXT_COLS, LANES), BF16),
            pltpu.VMEM((PAIRS, 2, RADIUS, COLS, LANES), BF16),
            pltpu.VMEM((PAIRS, 2, RADIUS, COLS, LANES), BF16),
            pltpu.VMEM((EXT_ROWS * SPAN, QN), F32),
            pltpu.VMEM((PAIRS, 2, EXT_ROWS // 2, 2, 2 * WIDE, LANES), BF16),
            pltpu.VMEM((PAIRS, 2, EXT_ROWS // 2, 2, 2 * WIDE, LANES), BF16),
            pltpu.VMEM((PAIRS, 2, EXT_ROWS // 2, 2, 2 * WIDE, LANES), BF16),
            pltpu.VMEM((PAIRS, 2, EXT_ROWS // 2, 2, 2 * WIDE, LANES), BF16),
            pltpu.VMEM((PAIRS, 2, 2, RADIUS, COLS, LANES), BF16),
            pltpu.VMEM((PAIRS, 2, 2, RADIUS, COLS, LANES), BF16),
            pltpu.VMEM((PAIRS, 2, EXT_ROWS, EXT_COLS, LANES), F32),
            pltpu.VMEM((2, EXT_ROWS * SPAN, 2 * QN), BF16),
            pltpu.VMEM((2, EXT_ROWS * SPAN, 2 * QN), BF16),
            pltpu.VMEM((2, EXT_ROWS * SPAN, 2 * QN), F32),
            pltpu.VMEM((2, 2, 8, 2 * QN), F32),
            pltpu.VMEM((PAIRS, 2, QN), F32),
            pltpu.VMEM((N_NEAR, 2 * PAIRS, QN), F32),
            pltpu.VMEM((N_FAR, 2 * PAIRS, QN), F32),
            dma(()),
            dma((4, PAIRS)),
            dma((PAIRS, 2, 2)),
            dma((PAIRS, 2, 2)),
            dma((PAIRS, 2, 3)),
            dma((PAIRS, 2, 3)),
            dma((PAIRS, 2, 3)),
            dma((PAIRS, 2, 3)),
            dma((PAIRS, 2)),
            dma((PAIRS, 2)),
            dma((N_NEAR,)),
            dma((N_NEAR,)),
            dma((N_FAR,)),
            dma((N_FAR,)),
            pltpu.SemaphoreType.REGULAR,
            pltpu.SemaphoreType.REGULAR,
        ],
        compiler_params=pltpu.CompilerParams(
            collective_id=0, has_side_effects=True, vmem_limit_bytes=60 * 1024 * 1024
        ),
    )(queries, keys, values, grad_out, sink_logits)
    results = [pltpu.with_memory_space_constraint(result, pltpu.VMEM) for result in results]
    return pl.pallas_call(
        place_results,
        out_shape=(shape,) * 4 + (jax.ShapeDtypeStruct((2 * PAIRS,), F32),),
        in_specs=[anywhere] * 4 + [vmem],
        out_specs=(anywhere,) * 4 + (vmem,),
        scratch_shapes=[dma((4,))],
    )(*results)


def solution(mesh):
    cells = P("lat", "lon", None)
    return jax.shard_map(
        on_device,
        mesh=mesh,
        in_specs=(cells,) * 4 + (P(),),
        out_specs=(cells,) * 4 + (P(),),
        check_vma=False,
    )
```

time: 62.5 us -> 46.4 us (0.74)
  Pallas kernels: 55.8 us -> 45.7 us
  local copies, waits for them, and re-layouts: 5.8 us -> 0 us
    pallas_call x1 -> x2, Pallas kernels: 55.8 us -> 45.7 us  [the longest x1 44.2 us: on_device(): pl.pallas_call(kernel, out_shape=(pltpu.VMEM(queries.shape, BF16),) * 4 +...]
    unnamed x12 -> x0, local copies, waits for them, and re-layouts: 5.18 us -> none
where the time goes in v2:
time: 46.4 us; the launch traced here: 46.3 us
  Pallas kernels  45.7 us (98%)
  between operations  0.64 us (1%)
    pallas_call x1, Pallas kernels, on_device(): pl.pallas_call(kernel, out_shape=(pltpu.VMEM(queries.shape, BF16),) * 4 +...  44.2 us
    pallas_call x1, Pallas kernels, on_device(): pl.pallas_call(place_results, out_shape=(shape,) * 4 + (jax.ShapeDtypeStr...  1.51 us

profile of v2, /device:TPU:1, one launch (start us, length us, event | category | flops | bytes accessed | tf_op | source)
XLA Modules:
  0.0 46.3 jit_solution(13422997651219436600)
XLA Ops:
  0.6 44.2 %shard_map.92 = (bf16[8,32,512]{2,1,0:T(8,128)(2,1)S(1)}, bf16[8,32,512]{2,1,0:T(8,128)(2,1)S(1)}, bf16[8,32,512]{2,1,0:T(8,128)(2,1)S(1)}, bf16[8,32,512]{2,1,0:T(8,128)(2,1)S(1)}, f32[8,128]{1,0:T(8,128)S(1)}) custom-call(bf16[8,32,512]{2,1,0:T(8,128)(2,1)} %q_hbm.1, bf16[8,32,512]{2,1,0:T(8,128)(2,1)} %k_hbm.1, bf16[8,32,512]{2,1,0:T(8,128)(2,1)} %v_hbm.1, ...), custom_call_target="tpu_custom_call" | custom-call | tf_op jit(solution)/shard_map/pallas_call | solution.py:550
  44.8 1.5 %shard_map.93 = (bf16[8,32,512]{2,1,0:T(8,128)(2,1)}, bf16[8,32,512]{2,1,0:T(8,128)(2,1)}, bf16[8,32,512]{2,1,0:T(8,128)(2,1)}, bf16[8,32,512]{2,1,0:T(8,128)(2,1)}, f32[8]{0:T(128)}) custom-call(bf16[8,32,512]{2,1,0:T(8,128)(2,1)S(1)} %get-tuple-element.10.o_ref, bf16[8,32,512]{2,1,0:T(8,128)(2,1)S(1)} %get-tuple-element.11.dq_ref, ...), custom_call_target="tpu_custom_call" | custom-call | tf_op jit(solution)/shard_map/pallas_call | solution.py:600

commit v3 on v2

--- a/solution.py
+++ b/solution.py
@@ -15,6 +15,7 @@
 ROWS = 8
 COLS = 32
 WIDE = 8
+CORNERS_FIRST = 2
 EXT_ROWS = ROWS + 2 * RADIUS
 EXT_COLS = COLS + 2 * WIDE
 TILE = 16
@@ -132,58 +133,6 @@
             greet(across(d, 0))
             greet(across(d, 1))
 
-    answers = ((core == 0) & jnp.logical_not(is_first)) | is_last
-    pl.semaphore_wait(barrier, N_NEAR + 2 * z + jnp.where(is_last, 3, jnp.where(answers, 1, 0)))
-
-    def lat_copy(p, i, side):
-        src = (k_hbm, v_hbm)[i]
-        first_row = (0, ROWS - RADIUS)[side]
-        return pltpu.make_async_remote_copy(
-            src_ref=src.at[
-                first_row : first_row + RADIUS, :, pl.ds(pl.multiple_of(p * LANES, LANES), LANES)
-            ],
-            dst_ref=(bot, top)[side].at[p, i],
-            send_sem=lat_send.at[p, i, side],
-            recv_sem=lat_recv.at[p, i, side],
-            device_id=(up, down)[side],
-            device_id_type=MESH,
-        )
-
-    def send_rows(p):
-        for i in range(2):
-            for side in range(2):
-                lat_copy(p, i, side).start()
-
-    send_rows(0)
-    send_rows(1)
-
-    @pl.when((core == 0) & jnp.logical_not(is_first))
-    def _():
-        pl.semaphore_signal(entered, inc=1, device_id=left, device_id_type=MESH)
-
-    @pl.when(is_last)
-    def _():
-        for da in (-1, 0, 1):
-            pl.semaphore_signal(entered, inc=1, device_id=diagonal(1, da), device_id_type=MESH)
-
-    for d in range(1, N_Z):
-        @pl.when(z - d >= 0)
-        def _():
-            for dh in range(2):
-                pl.semaphore_signal(met, inc=1, device_id=across(-d, dh), device_id_type=MESH)
-
-    key = lax.broadcasted_iota(jnp.int32, (EXT_ROWS * SPAN, QN), 0)
-    query = lax.broadcasted_iota(jnp.int32, (EXT_ROWS * SPAN, QN), 1)
-    key_row = key // SPAN - RADIUS
-    row_gap = key_row - query // TILE
-    col_gap = lax.rem(key, SPAN) - WIDE - lax.rem(query, TILE)
-    whole_row = a * ROWS + key_row
-    meets = (
-        (row_gap >= -RADIUS) & (row_gap <= RADIUS) & (col_gap >= -RADIUS) & (col_gap <= RADIUS)
-        & (whole_row >= 0) & (whole_row < N_LAT * ROWS)
-    )
-    mask[...] = jnp.where(meets, 1.0, 0.0)
-
     def rows_of(p, i, r):
         if r < RADIUS:
             return top[p, i, r].astype(F32)
@@ -201,6 +150,7 @@
                 ).astype(BF16)
 
     spans = ((3, 4), (0, 3), (7, 3))
+
     direct = (is_first, is_last)
 
     def strip_copy(p, side, part):
@@ -225,20 +175,79 @@
             load(i, p).wait()
         pack(p, 3, 7)
 
+    answers = ((core == 0) & jnp.logical_not(is_first)) | is_last
+    pl.semaphore_wait(barrier, N_NEAR + 2 * z + jnp.where(is_last, 3, jnp.where(answers, 1, 0)))
+
+    def lat_copy(p, i, side):
+        src = (k_hbm, v_hbm)[i]
+        first_row = (0, ROWS - RADIUS)[side]
+        return pltpu.make_async_remote_copy(
+            src_ref=src.at[
+                first_row : first_row + RADIUS, :, pl.ds(pl.multiple_of(p * LANES, LANES), LANES)
+            ],
+            dst_ref=(bot, top)[side].at[p, i],
+            send_sem=lat_send.at[p, i, side],
+            recv_sem=lat_recv.at[p, i, side],
+            device_id=(up, down)[side],
+            device_id_type=MESH,
+        )
+
+    def send_rows(p):
+        for i in range(2):
+            for side in range(2):
+                lat_copy(p, i, side).start()
+
+    def send_corners(side, first, last):
+        for p in range(first, last):
+            for part in (1, 2):
+                strip_copy(p, side, part).start()
+
+    sure = ((core == 1) | jnp.logical_not(is_first), (core == 0) | is_last)
+
     @pl.when(is_last)
     def _():
-        for p in range(PAIRS):
-            for part in (1, 2):
-                strip_copy(p, 1, part).start()
-
-    send_rows(2)
-    send_rows(3)
-    sure = ((core == 1) | (core == 0) & jnp.logical_not(is_first), (core == 0) | is_last)
+        send_corners(1, 0, CORNERS_FIRST)
+
+    send_rows(0)
     for side in range(2):
         @pl.when(sure[side])
         def _():
             for p in range(PAIRS):
                 strip_copy(p, side, 0).start()
+
+    @pl.when(is_last)
+    def _():
+        send_corners(1, CORNERS_FIRST, PAIRS)
+
+    for p in range(1, PAIRS):
+        send_rows(p)
+
+    @pl.when((core == 0) & jnp.logical_not(is_first))
+    def _():
+        pl.semaphore_signal(entered, inc=1, device_id=left, device_id_type=MESH)
+
+    @pl.when(is_last)
+    def _():
+        for da in (-1, 0, 1):
+            pl.semaphore_signal(entered, inc=1, device_id=diagonal(1, da), device_id_type=MESH)
+
+    for d in range(1, N_Z):
+        @pl.when(z - d >= 0)
+        def _():
+            for dh in range(2):
+                pl.semaphore_signal(met, inc=1, device_id=across(-d, dh), device_id_type=MESH)
+
+    key = lax.broadcasted_iota(jnp.int32, (EXT_ROWS * SPAN, QN), 0)
+    query = lax.broadcasted_iota(jnp.int32, (EXT_ROWS * SPAN, QN), 1)
+    key_row = key // SPAN - RADIUS
+    row_gap = key_row - query // TILE
+    col_gap = lax.rem(key, SPAN) - WIDE - lax.rem(query, TILE)
+    whole_row = a * ROWS + key_row
+    meets = (
+        (row_gap >= -RADIUS) & (row_gap <= RADIUS) & (col_gap >= -RADIUS) & (col_gap <= RADIUS)
+        & (whole_row >= 0) & (whole_row < N_LAT * ROWS)
+    )
+    mask[...] = jnp.where(meets, 1.0, 0.0)
 
     acc[...] = jnp.zeros_like(acc)
     sk[...] = jnp.zeros_like(sk)
@@ -485,12 +494,14 @@
     lax.fori_loop(0, PAIRS - 1, step, 0)
     gather(PAIRS - 1)
     forward_both(PAIRS - 1)
-    sk_plane[0] = sk[...].reshape(2 * PAIRS, QN)
+    heads = jnp.sum(sk[...].reshape(2 * PAIRS, QN), axis=1, keepdims=True)
+    row = lax.broadcasted_iota(jnp.int32, (2 * PAIRS, QN), 0)
+    column_of = lax.broadcasted_iota(jnp.int32, (2 * PAIRS, QN), 1)
+    sk_plane[0] = jnp.sum(jnp.where(row == column_of, heads, 0.0), axis=0, keepdims=True)
     for d in range(1, N_NEAR):
         skp_copy(d).start()
     backward_both(PAIRS - 1)
     stage_c(PAIRS - 2)
-    stage_c(PAIRS - 1)
     for d in range(1, N_NEAR):
         skp_copy(d).wait_recv()
     sk_z[0] = jnp.sum(sk_plane[...], axis=0)
@@ -502,6 +513,8 @@
     for d in range(1, N_FAR):
         skz_copy(d).start()
 
+    stage_c(PAIRS - 1)
+
     def finish(p, carry):
         stage_d(p)
         return carry
@@ -509,9 +522,7 @@
     lax.fori_loop(0, PAIRS, finish, 0)
     for d in range(1, N_FAR):
         skz_copy(d).wait_recv()
-    sg_ref[...] = jnp.broadcast_to(
-        jnp.sum(jnp.sum(sk_z[...], axis=0), axis=1, keepdims=True), (2 * PAIRS, QN)
-    )
+    sg_ref[...] = jnp.sum(sk_z[...], axis=0)
 
     for p in range(PAIRS):
         for side in range(2):
@@ -535,9 +546,7 @@
     ]
     for store in stores:
         store.start()
-    row = lax.broadcasted_iota(jnp.int32, (2 * PAIRS, QN), 0)
-    lane = lax.broadcasted_iota(jnp.int32, (2 * PAIRS, QN), 1)
-    sg_out[...] = jnp.sum(jnp.where(row == lane, sg_ref[...], 0.0), axis=0)[: 2 * PAIRS]
+    sg_out[...] = sg_ref[0, : 2 * PAIRS]
     for store in stores:
         store.wait()
 
@@ -549,7 +558,7 @@
     vmem = pl.BlockSpec(memory_space=pltpu.VMEM)
     results = pl.pallas_call(
         kernel,
-        out_shape=(pltpu.VMEM(queries.shape, BF16),) * 4 + (pltpu.VMEM((2 * PAIRS, QN), F32),),
+        out_shape=(pltpu.VMEM(queries.shape, BF16),) * 4 + (pltpu.VMEM((1, QN), F32),),
         in_specs=[anywhere] * 5,
         out_specs=(vmem,) * 5,
         scratch_shapes=[
@@ -573,8 +582,8 @@
             pltpu.VMEM((2, EXT_ROWS * SPAN, 2 * QN), F32),
             pltpu.VMEM((2, 2, 8, 2 * QN), F32),
             pltpu.VMEM((PAIRS, 2, QN), F32),
-            pltpu.VMEM((N_NEAR, 2 * PAIRS, QN), F32),
-            pltpu.VMEM((N_FAR, 2 * PAIRS, QN), F32),
+            pltpu.VMEM((N_NEAR, 1, QN), F32),
+            pltpu.VMEM((N_FAR, 1, QN), F32),
             dma(()),
             dma((4, PAIRS)),
             dma((PAIRS, 2, 2)),

time: 46.4 us -> 41.8 us (0.901)
  Pallas kernels: 45.7 us -> 41 us
    pallas_call x1, Pallas kernels: 44.2 us -> 39.5 us  [on_device(): pl.pallas_call(kernel, out_shape=(pltpu.VMEM(queries.shape, BF16),) * 4 +...]
where the time goes in v3:
time: 41.8 us; the launch traced here: 41.7 us
  Pallas kernels  41 us (98%)
  between operations  0.64 us (2%)
    pallas_call x1, Pallas kernels, on_device(): pl.pallas_call(kernel, out_shape=(pltpu.VMEM(queries.shape, BF16),) * 4 +...  39.5 us
    pallas_call x1, Pallas kernels, on_device(): pl.pallas_call(place_results, out_shape=(shape,) * 4 + (jax.ShapeDtypeStr...  1.51 us

profile of v3, /device:TPU:1, one launch (start us, length us, event | category | flops | bytes accessed | tf_op | source)
XLA Modules:
  0.0 41.7 jit_solution(7001696360503960464)
XLA Ops:
  0.6 39.5 %shard_map.92 = (bf16[8,32,512]{2,1,0:T(8,128)(2,1)S(1)}, bf16[8,32,512]{2,1,0:T(8,128)(2,1)S(1)}, bf16[8,32,512]{2,1,0:T(8,128)(2,1)S(1)}, bf16[8,32,512]{2,1,0:T(8,128)(2,1)S(1)}, f32[1,128]{1,0:T(1,128)S(1)}) custom-call(bf16[8,32,512]{2,1,0:T(8,128)(2,1)} %q_hbm.1, bf16[8,32,512]{2,1,0:T(8,128)(2,1)} %k_hbm.1, bf16[8,32,512]{2,1,0:T(8,128)(2,1)} %v_hbm.1, ...), custom_call_target="tpu_custom_call" | custom-call | tf_op jit(solution)/shard_map/pallas_call | solution.py:559
  40.2 1.5 %shard_map.93 = (bf16[8,32,512]{2,1,0:T(8,128)(2,1)}, bf16[8,32,512]{2,1,0:T(8,128)(2,1)}, bf16[8,32,512]{2,1,0:T(8,128)(2,1)}, bf16[8,32,512]{2,1,0:T(8,128)(2,1)}, f32[8]{0:T(128)}) custom-call(bf16[8,32,512]{2,1,0:T(8,128)(2,1)S(1)} %get-tuple-element.10.o_ref, bf16[8,32,512]{2,1,0:T(8,128)(2,1)S(1)} %get-tuple-element.11.dq_ref, ...), custom_call_target="tpu_custom_call" | custom-call | tf_op jit(solution)/shard_map/pallas_call | solution.py:609

commit v4 on v3

--- a/solution.py
+++ b/solution.py
@@ -178,6 +178,18 @@
     answers = ((core == 0) & jnp.logical_not(is_first)) | is_last
     pl.semaphore_wait(barrier, N_NEAR + 2 * z + jnp.where(is_last, 3, jnp.where(answers, 1, 0)))
 
+    goes = (a > 0, a < N_LAT - 1)
+
+    @pl.when(a == 0)
+    def _():
+        top[...] = jnp.zeros_like(top)
+        rim_from[:, 0] = jnp.zeros((PAIRS, 2, RADIUS, COLS, LANES), BF16)
+
+    @pl.when(a == N_LAT - 1)
+    def _():
+        bot[...] = jnp.zeros_like(bot)
+        rim_from[:, 1] = jnp.zeros((PAIRS, 2, RADIUS, COLS, LANES), BF16)
+
     def lat_copy(p, i, side):
         src = (k_hbm, v_hbm)[i]
         first_row = (0, ROWS - RADIUS)[side]
@@ -193,9 +205,11 @@
         )
 
     def send_rows(p):
-        for i in range(2):
-            for side in range(2):
-                lat_copy(p, i, side).start()
+        for side in range(2):
+            @pl.when(goes[side])
+            def _():
+                for i in range(2):
+                    lat_copy(p, i, side).start()
 
     def send_corners(side, first, last):
         for p in range(first, last):
@@ -253,9 +267,11 @@
     sk[...] = jnp.zeros_like(sk)
 
     def stage_a(p):
-        for i in range(2):
-            for side in range(2):
-                lat_copy(p, i, side).wait_recv()
+        for side in range(2):
+            @pl.when(goes[1 - side])
+            def _():
+                for i in range(2):
+                    lat_copy(p, i, side).wait_recv()
         pack(p, 0, 3)
         pack(p, 7, 10)
         for side in range(2):
@@ -399,7 +415,9 @@
                 rim_to[p, 0, i, r] = acc[p, i, r, WIDE : WIDE + COLS, :].astype(BF16)
                 rim_to[p, 1, i, r] = acc[p, i, RADIUS + ROWS + r, WIDE : WIDE + COLS, :].astype(BF16)
         for side in range(2):
-            rim_copy(p, side).start()
+            @pl.when(goes[side])
+            def _():
+                rim_copy(p, side).start()
 
     def stage_d(p):
         for side in range(2):
@@ -415,7 +433,9 @@
                     add_strip(p, side, rp, 2 * rp + RADIUS)
                     add_strip(p, side, rp + 7, 2 * rp + RADIUS + 2)
         for side in range(2):
-            rim_copy(p, side).wait_recv()
+            @pl.when(goes[1 - side])
+            def _():
+                rim_copy(p, side).wait_recv()
         for i in range(2):
             for r in range(ROWS):
                 total = acc[p, i, RADIUS + r, WIDE : WIDE + COLS, :]
@@ -526,12 +546,14 @@
 
     for p in range(PAIRS):
         for side in range(2):
-            for i in range(2):
-                lat_copy(p, i, side).wait_send()
+            @pl.when(goes[side])
+            def _():
+                rim_copy(p, side).wait_send()
+                for i in range(2):
+                    lat_copy(p, i, side).wait_send()
             for part in range(3):
                 strip_copy(p, side, part).wait_send()
                 gs_copy(p, side, part).wait_send()
-            rim_copy(p, side).wait_send()
     for d in range(1, N_NEAR):
         skp_copy(d).wait_send()
     for d in range(1, N_FAR):

time: 41.8 us -> 40.7 us (0.974)
  Pallas kernels: 41 us -> 39.9 us
    pallas_call x1, Pallas kernels: 39.5 us -> 38.4 us  [on_device(): pl.pallas_call(kernel, out_shape=(pltpu.VMEM(queries.shape, BF16),) * 4 +...]
where the time goes in v4:
time: 40.7 us; the launch traced here: 40.6 us
  Pallas kernels  39.9 us (98%)
  between operations  0.64 us (2%)
    pallas_call x1, Pallas kernels, on_device(): pl.pallas_call(kernel, out_shape=(pltpu.VMEM(queries.shape, BF16),) * 4 +...  38.4 us
    pallas_call x1, Pallas kernels, on_device(): pl.pallas_call(place_results, out_shape=(shape,) * 4 + (jax.ShapeDtypeStr...  1.51 us

profile of v4, /device:TPU:1, one launch (start us, length us, event | category | flops | bytes accessed | tf_op | source)
XLA Modules:
  0.0 40.6 jit_solution(714618621737841462)
XLA Ops:
  0.6 38.4 %shard_map.92 = (bf16[8,32,512]{2,1,0:T(8,128)(2,1)S(1)}, bf16[8,32,512]{2,1,0:T(8,128)(2,1)S(1)}, bf16[8,32,512]{2,1,0:T(8,128)(2,1)S(1)}, bf16[8,32,512]{2,1,0:T(8,128)(2,1)S(1)}, f32[1,128]{1,0:T(1,128)S(1)}) custom-call(bf16[8,32,512]{2,1,0:T(8,128)(2,1)} %q_hbm.1, bf16[8,32,512]{2,1,0:T(8,128)(2,1)} %k_hbm.1, bf16[8,32,512]{2,1,0:T(8,128)(2,1)} %v_hbm.1, ...), custom_call_target="tpu_custom_call" | custom-call | tf_op jit(solution)/shard_map/pallas_call | solution.py:581
  39.1 1.5 %shard_map.93 = (bf16[8,32,512]{2,1,0:T(8,128)(2,1)}, bf16[8,32,512]{2,1,0:T(8,128)(2,1)}, bf16[8,32,512]{2,1,0:T(8,128)(2,1)}, bf16[8,32,512]{2,1,0:T(8,128)(2,1)}, f32[8]{0:T(128)}) custom-call(bf16[8,32,512]{2,1,0:T(8,128)(2,1)S(1)} %get-tuple-element.10.o_ref, bf16[8,32,512]{2,1,0:T(8,128)(2,1)S(1)} %get-tuple-element.11.dq_ref, ...), custom_call_target="tpu_custom_call" | custom-call | tf_op jit(solution)/shard_map/pallas_call | solution.py:631
